TPU v7x, 128 devices: a whole 4x4x4 slice. The times are simulated.
128 devices in a mesh: query: 8 (over y, core), space: 16 (over x, z).
Axes of the slice: x: 4, y: 4, z: 4, core: 2. Of those that a mesh axis runs over, the one named last changes fastest.
Arguments:
- queries: bfloat16 [4096, 256], P('query'), may hold values from -34 to 34
- features: bfloat16 [131072, 256], P(('space', 'query')), may hold values from -6 to 6
- block_lists: int32 [64, 46], replicated, may hold values from 0 to 1023, as said below
- w_query: bfloat16 [256, 256], replicated, may hold values from -1 to 1
- w_key: bfloat16 [256, 256], replicated, may hold values from -0.375 to 0.375
- w_value: bfloat16 [256, 256], replicated, may hold values from -0.375 to 0.375
- w_out: bfloat16 [256, 256], replicated, may hold values from -0.375 to 0.375
- norm_gain: float32 [256], replicated, may hold values from 0.1 to 1.9
- w_mask: bfloat16 [256, 256], replicated, may hold values from -0.375 to 0.375
Outputs:
- new_queries: bfloat16 [4096, 256], P('query')
- mask_logits: float32 [4096, 131072], P('query', 'space')
Inputs may be any that keep to these rules, and one draw needn't show every extreme that they name: `block_lists`: each row names 46 distinct superpoint blocks, of which exactly 16 lie on one space index (block g lies on index g // 64) and exactly 2 on each other index; among the 8 rows k * 8 to k * 8 + 7, for k from 1 to 7, these busiest indices are all different.
All inputs are finite; a program needn't handle non-finite values.
Results may differ from a plain program's by a relative error of at most 0.012.
Values may be sent and summed in bfloat16 or wider, within the bound.
No kernel may reach another device: no remote copies, remote signals or barrier semaphores. Data moves between devices by JAX's collectives and lax.ppermute only.
A program may use at most 128 MiB of HBM per device.

v0:
```python
import math

import jax
import jax.numpy as jnp
from jax import lax
from jax.sharding import PartitionSpec as P

D = 256
H = 8
HD = 32
QBLK = 64
SBLK = 128
CAP = 16


def merged(part, axis, combine):
    gathered = jax.tree.map(lambda a: lax.all_gather(a, axis), part)

    def take(source):
        return jax.tree.map(lambda a: lax.dynamic_index_in_dim(a, source, 0, False), gathered)

    return lax.fori_loop(
        1, lax.axis_size(axis), lambda source, state: combine(state, take(source)), take(0)
    )


def layer_norm(rows, gain):
    center = rows - jnp.mean(rows, axis=-1, keepdims=True)
    spread = jnp.mean(center * center, axis=-1, keepdims=True)
    return center * lax.rsqrt(spread + 1e-05) * gain


def join_partials(first, second):
    highest = jnp.maximum(first[0], second[0])
    first_factor = jnp.exp(first[0] - highest)
    second_factor = jnp.exp(second[0] - highest)
    totals = first[1] * first_factor + second[1] * second_factor
    mixed = first[2] * jnp.repeat(first_factor, HD, axis=1) + second[2] * jnp.repeat(
        second_factor, HD, axis=1
    )
    return (highest, totals, mixed)


def finish_rows(sums, totals, query_rows, w_out, norm_gain, w_mask):
    count = sums.shape[0]
    heads_out = (
        (sums.reshape(count, H, HD) / totals[:, :, None]).reshape(count, D).astype(jnp.bfloat16)
    )
    residual = query_rows.astype(jnp.float32) + jnp.dot(
        heads_out, w_out, preferred_element_type=jnp.float32
    )
    updated = layer_norm(residual, norm_gain).astype(jnp.bfloat16)
    embedded = jnp.dot(updated, w_mask, preferred_element_type=jnp.float32).astype(jnp.bfloat16)
    return (updated, embedded)


def shards(queries, features, block_lists, w_query, w_key, w_value, w_out, norm_gain, w_mask):
    score_scale = 1.0 / math.sqrt(HD)
    whole_features = lax.all_gather(features, "query", axis=0, tiled=True)
    key_rows = jnp.dot(whole_features, w_key, preferred_element_type=jnp.float32).astype(
        jnp.bfloat16
    )
    value_rows = jnp.dot(whole_features, w_value, preferred_element_type=jnp.float32).astype(
        jnp.bfloat16
    )
    block_count = whole_features.shape[0] // SBLK
    key_blocks = key_rows.reshape(block_count, SBLK, D)
    value_blocks = value_rows.reshape(block_count, SBLK, D)
    blocks_here = queries.shape[0] // QBLK
    list_width = block_lists.shape[1]
    space_rank = lax.axis_index("space")
    query_rank = lax.axis_index("query")
    my_lists = lax.dynamic_slice_in_dim(block_lists, query_rank * blocks_here, blocks_here, 0)
    is_local = my_lists // block_count == space_rank
    local_ids = my_lists % block_count
    query_proj = jnp.dot(queries, w_query, preferred_element_type=jnp.float32).astype(jnp.bfloat16)
    query_heads = query_proj.reshape(blocks_here, QBLK, H, HD)
    places = jnp.arange(list_width, dtype=jnp.int32)[None, :]
    ranking = jnp.argsort(jnp.where(is_local, places, places + list_width), axis=1)[:, :CAP]
    live_all = jnp.take_along_axis(is_local, ranking, 1)
    chosen_all = jnp.where(live_all, jnp.take_along_axis(local_ids, ranking, 1), 0)

    def block_partials(item):
        heads, chosen, live_slots = item
        picked_keys = key_blocks[chosen].reshape(-1, H, HD)
        picked_values = value_blocks[chosen].reshape(-1, H, HD)
        keep = jnp.broadcast_to(live_slots[:, None], (live_slots.shape[0], SBLK)).reshape(-1)
        scores = (
            jnp.einsum("qhd,khd->hqk", heads, picked_keys, preferred_element_type=jnp.float32)
            * score_scale
        )
        scores = jnp.where(keep, scores, -1e30)
        block_max = jnp.max(scores, axis=-1)
        numerators = jnp.where(keep, jnp.exp(scores - block_max[:, :, None]), 0.0)
        block_totals = jnp.sum(numerators, axis=-1)
        block_mixed = jnp.einsum(
            "hqk,khd->qhd",
            numerators.astype(jnp.bfloat16),
            picked_values,
            preferred_element_type=jnp.float32,
        )
        return (jnp.transpose(block_max), jnp.transpose(block_totals), block_mixed.reshape(QBLK, D))

    highest, totals, mixed = lax.map(block_partials, (query_heads, chosen_all, live_all))
    highest = highest.reshape(-1, H)
    totals = totals.reshape(-1, H)
    mixed = mixed.reshape(-1, D)
    highest, totals, mixed = merged((highest, totals, mixed), "space", join_partials)
    updated, embedded = finish_rows(mixed, totals, queries, w_out, norm_gain, w_mask)
    mask_scale = 1.0 / math.sqrt(D)
    mask_logits = (
        jnp.einsum("qd,sd->qs", embedded, whole_features, preferred_element_type=jnp.float32)
        * mask_scale
    )
    return (updated, mask_logits)


def solution(mesh):
    placed = (P("query", None), P(("space", "query"), None), P(), P(), P(), P(), P(), P(), P())
    return jax.shard_map(
        shards,
        mesh=mesh,
        in_specs=placed,
        out_specs=(P("query", None), P("query", "space")),
        check_vma=False,
    )
```

profile of v0, /device:TPU:0, one launch (start us, length us, event | category | flops | bytes accessed | tf_op | source)
XLA Modules:
  0.0 321.5 jit_solution(11525978522403889763)
XLA Ops:
  15.0 29.4 %all-gather.3.cloned.1.call-done = bf16[8192,256]{1,0:T(8,128)(2,1)} async-done(((bf16[1024,256]{1,0:T(8,128)(2,1)}), bf16[8192,256]{1,0:T(8,128)(2,1)}) %all-gather.3.cloned.1.call-update) | async-done | bytes 4194320 | tf_op jit(solution)/shard_map/all_gather | solution.py:59
  44.4 5.6 %convolution_convert_fusion.1 = bf16[8192,256]{1,0:T(8,128)(2,1)} fusion(bf16[8192,256]{1,0:T(8,128)(2,1)} %all-gather.3.cloned.1.call-done, bf16[256,256]{1,0:T(8,128)(2,1)S(1)} %copy-done.3), kind=kOutput, calls=%fused_computation.38 | convolution fusion | flops 1075838976 | bytes 8519680 | tf_op jit(solution)/shard_map/dot_general | solution.py:60
  50.0 3.2 convolution_convert_fusion
  53.2 153.0 %while.33 = (s32[]{:T(128)}, f32[8,64,8]{1,0,2:T(8,128)S(1)}, f32[8,64,8]{1,0,2:T(8,128)S(1)}, f32[8,64,256]{2,1,0:T(8,128)}, pred[8,16]{1,0:T(8,128)(4,1)S(1)},...) while((s32[]{:T(128)}, f32[8,64,8]{1,0,2:T(8,128)S(1)}, ...), condition=%wide.region_4.5_spmd, body=%wide.region_1.4_spmd.sunk | while | flops 147849264 | bytes 27685872 | solution.py:104
  57.7 2.8 fusion.51
  64.9 3.3 %fusion.53 = f32[8,32,64]{2,1,0:T(8,128)S(1)} fusion(bf16[2048,8,32]{0,2,1:T(8,128)(2,1)S(1)} %reshape.156, f32[8,64,2048]{2,1,0:T(8,128)} %get-tuple-element.437, f32[8,64]{1,0:T(8,128)S(1)} %get-tuple-element.436, pred[2048]{0:T(1024)(128)(4,1)S(1)} %broadcast_bitcast_fusion.2), kind=kOutput, calls=%fused_computation.19.clone.1 | convolution fusion | flops 72351744 | bytes 5312512 | tf_op jit(solution)/shard_map/while/body/eval_jaxpr/hqk,khd->qhd/dot_general | solution.py:96
  68.9 3.3 %fusion.52 = f32[8,64]{1,0:T(8,128)S(1)} fusion(f32[8,64,2048]{2,1,0:T(8,128)} %get-tuple-element.437, f32[8,64]{1,0:T(8,128)S(1)} %get-tuple-element.436, pred[2048]{0:T(1024)(128)(4,1)S(1)} %broadcast_bitcast_fusion.2), kind=kLoop, calls=%fused_computation.18.clone.1 | loop fusion | flops 5242368 | bytes 4200448 | tf_op jit(solution)/shard_map/while/body/eval_jaxpr/reduce_sum | solution.py:95
  76.8 2.8 fusion.51
  84.1 3.3 %fusion.53 = f32[8,32,64]{2,1,0:T(8,128)S(1)} fusion(bf16[2048,8,32]{0,2,1:T(8,128)(2,1)S(1)} %reshape.156, f32[8,64,2048]{2,1,0:T(8,128)} %get-tuple-element.437, f32[8,64]{1,0:T(8,128)S(1)} %get-tuple-element.436, pred[2048]{0:T(1024)(128)(4,1)S(1)} %broadcast_bitcast_fusion.2), kind=kOutput, calls=%fused_computation.19.clone.1 | convolution fusion | flops 72351744 | bytes 5312512 | tf_op jit(solution)/shard_map/while/body/eval_jaxpr/hqk,khd->qhd/dot_general | solution.py:96
  88.1 3.3 %fusion.52 = f32[8,64]{1,0:T(8,128)S(1)} fusion(f32[8,64,2048]{2,1,0:T(8,128)} %get-tuple-element.437, f32[8,64]{1,0:T(8,128)S(1)} %get-tuple-element.436, pred[2048]{0:T(1024)(128)(4,1)S(1)} %broadcast_bitcast_fusion.2), kind=kLoop, calls=%fused_computation.18.clone.1 | loop fusion | flops 5242368 | bytes 4200448 | tf_op jit(solution)/shard_map/while/body/eval_jaxpr/reduce_sum | solution.py:95
  96.0 2.8 fusion.51
  103.2 3.3 %fusion.53 = f32[8,32,64]{2,1,0:T(8,128)S(1)} fusion(bf16[2048,8,32]{0,2,1:T(8,128)(2,1)S(1)} %reshape.156, f32[8,64,2048]{2,1,0:T(8,128)} %get-tuple-element.437, f32[8,64]{1,0:T(8,128)S(1)} %get-tuple-element.436, pred[2048]{0:T(1024)(128)(4,1)S(1)} %broadcast_bitcast_fusion.2), kind=kOutput, calls=%fused_computation.19.clone.1 | convolution fusion | flops 72351744 | bytes 5312512 | tf_op jit(solution)/shard_map/while/body/eval_jaxpr/hqk,khd->qhd/dot_general | solution.py:96
  107.2 3.3 %fusion.52 = f32[8,64]{1,0:T(8,128)S(1)} fusion(f32[8,64,2048]{2,1,0:T(8,128)} %get-tuple-element.437, f32[8,64]{1,0:T(8,128)S(1)} %get-tuple-element.436, pred[2048]{0:T(1024)(128)(4,1)S(1)} %broadcast_bitcast_fusion.2), kind=kLoop, calls=%fused_computation.18.clone.1 | loop fusion | flops 5242368 | bytes 4200448 | tf_op jit(solution)/shard_map/while/body/eval_jaxpr/reduce_sum | solution.py:95
  115.1 2.8 fusion.51
  122.3 3.3 %fusion.53 = f32[8,32,64]{2,1,0:T(8,128)S(1)} fusion(bf16[2048,8,32]{0,2,1:T(8,128)(2,1)S(1)} %reshape.156, f32[8,64,2048]{2,1,0:T(8,128)} %get-tuple-element.437, f32[8,64]{1,0:T(8,128)S(1)} %get-tuple-element.436, pred[2048]{0:T(1024)(128)(4,1)S(1)} %broadcast_bitcast_fusion.2), kind=kOutput, calls=%fused_computation.19.clone.1 | convolution fusion | flops 72351744 | bytes 5312512 | tf_op jit(solution)/shard_map/while/body/eval_jaxpr/hqk,khd->qhd/dot_general | solution.py:96
  126.3 3.3 %fusion.52 = f32[8,64]{1,0:T(8,128)S(1)} fusion(f32[8,64,2048]{2,1,0:T(8,128)} %get-tuple-element.437, f32[8,64]{1,0:T(8,128)S(1)} %get-tuple-element.436, pred[2048]{0:T(1024)(128)(4,1)S(1)} %broadcast_bitcast_fusion.2), kind=kLoop, calls=%fused_computation.18.clone.1 | loop fusion | flops 5242368 | bytes 4200448 | tf_op jit(solution)/shard_map/while/body/eval_jaxpr/reduce_sum | solution.py:95
  134.2 2.8 fusion.51
  141.5 3.3 %fusion.53 = f32[8,32,64]{2,1,0:T(8,128)S(1)} fusion(bf16[2048,8,32]{0,2,1:T(8,128)(2,1)S(1)} %reshape.156, f32[8,64,2048]{2,1,0:T(8,128)} %get-tuple-element.437, f32[8,64]{1,0:T(8,128)S(1)} %get-tuple-element.436, pred[2048]{0:T(1024)(128)(4,1)S(1)} %broadcast_bitcast_fusion.2), kind=kOutput, calls=%fused_computation.19.clone.1 | convolution fusion | flops 72351744 | bytes 5312512 | tf_op jit(solution)/shard_map/while/body/eval_jaxpr/hqk,khd->qhd/dot_general | solution.py:96
  145.5 3.3 %fusion.52 = f32[8,64]{1,0:T(8,128)S(1)} fusion(f32[8,64,2048]{2,1,0:T(8,128)} %get-tuple-element.437, f32[8,64]{1,0:T(8,128)S(1)} %get-tuple-element.436, pred[2048]{0:T(1024)(128)(4,1)S(1)} %broadcast_bitcast_fusion.2), kind=kLoop, calls=%fused_computation.18.clone.1 | loop fusion | flops 5242368 | bytes 4200448 | tf_op jit(solution)/shard_map/while/body/eval_jaxpr/reduce_sum | solution.py:95
  160.6 3.3 %fusion.53 = f32[8,32,64]{2,1,0:T(8,128)S(1)} fusion(bf16[2048,8,32]{0,2,1:T(8,128)(2,1)S(1)} %reshape.156, f32[8,64,2048]{2,1,0:T(8,128)} %get-tuple-element.437, f32[8,64]{1,0:T(8,128)S(1)} %get-tuple-element.436, pred[2048]{0:T(1024)(128)(4,1)S(1)} %broadcast_bitcast_fusion.2), kind=kOutput, calls=%fused_computation.19.clone.1 | convolution fusion | flops 72351744 | bytes 5312512 | tf_op jit(solution)/shard_map/while/body/eval_jaxpr/hqk,khd->qhd/dot_general | solution.py:96
  164.6 3.3 %fusion.52 = f32[8,64]{1,0:T(8,128)S(1)} fusion(f32[8,64,2048]{2,1,0:T(8,128)} %get-tuple-element.437, f32[8,64]{1,0:T(8,128)S(1)} %get-tuple-element.436, pred[2048]{0:T(1024)(128)(4,1)S(1)} %broadcast_bitcast_fusion.2), kind=kLoop, calls=%fused_computation.18.clone.1 | loop fusion | flops 5242368 | bytes 4200448 | tf_op jit(solution)/shard_map/while/body/eval_jaxpr/reduce_sum | solution.py:95
  172.5 2.8 fusion.51
  179.7 3.3 %fusion.53 = f32[8,32,64]{2,1,0:T(8,128)S(1)} fusion(bf16[2048,8,32]{0,2,1:T(8,128)(2,1)S(1)} %reshape.156, f32[8,64,2048]{2,1,0:T(8,128)} %get-tuple-element.437, f32[8,64]{1,0:T(8,128)S(1)} %get-tuple-element.436, pred[2048]{0:T(1024)(128)(4,1)S(1)} %broadcast_bitcast_fusion.2), kind=kOutput, calls=%fused_computation.19.clone.1 | convolution fusion | flops 72351744 | bytes 5312512 | tf_op jit(solution)/shard_map/while/body/eval_jaxpr/hqk,khd->qhd/dot_general | solution.py:96
  183.7 3.3 %fusion.52 = f32[8,64]{1,0:T(8,128)S(1)} fusion(f32[8,64,2048]{2,1,0:T(8,128)} %get-tuple-element.437, f32[8,64]{1,0:T(8,128)S(1)} %get-tuple-element.436, pred[2048]{0:T(1024)(128)(4,1)S(1)} %broadcast_bitcast_fusion.2), kind=kLoop, calls=%fused_computation.18.clone.1 | loop fusion | flops 5242368 | bytes 4200448 | tf_op jit(solution)/shard_map/while/body/eval_jaxpr/reduce_sum | solution.py:95
  191.6 2.8 fusion.51
  198.9 3.3 %fusion.53 = f32[8,32,64]{2,1,0:T(8,128)S(1)} fusion(bf16[2048,8,32]{0,2,1:T(8,128)(2,1)S(1)} %reshape.156, f32[8,64,2048]{2,1,0:T(8,128)} %get-tuple-element.437, f32[8,64]{1,0:T(8,128)S(1)} %get-tuple-element.436, pred[2048]{0:T(1024)(128)(4,1)S(1)} %broadcast_bitcast_fusion.2), kind=kOutput, calls=%fused_computation.19.clone.1 | convolution fusion | flops 72351744 | bytes 5312512 | tf_op jit(solution)/shard_map/while/body/eval_jaxpr/hqk,khd->qhd/dot_general | solution.py:96
  202.9 3.3 %fusion.52 = f32[8,64]{1,0:T(8,128)S(1)} fusion(f32[8,64,2048]{2,1,0:T(8,128)} %get-tuple-element.437, f32[8,64]{1,0:T(8,128)S(1)} %get-tuple-element.436, pred[2048]{0:T(1024)(128)(4,1)S(1)} %broadcast_bitcast_fusion.2), kind=kLoop, calls=%fused_computation.18.clone.1 | loop fusion | flops 5242368 | bytes 4200448 | tf_op jit(solution)/shard_map/while/body/eval_jaxpr/reduce_sum | solution.py:95
  206.6 24.2 %all_gather.14 = f32[16,512,8]{1,2,0:T(8,128)S(1)} all-gather(f32[1,512,8]{1,2,0:T(8,128)S(1)} %all_gather_reshape.10), channel_id=1, replica_groups=mesh['query'=8,'space'=16] {'space'}, dimensions={0}, use_global_device_ids=true | all-gather | bytes 278528 | tf_op jit(solution)/shard_map/all_gather | solution.py:17
  230.8 23.7 %all_gather.13 = f32[16,512,8]{1,2,0:T(8,128)S(1)} all-gather(f32[1,512,8]{1,2,0:T(8,128)S(1)} %all_gather_reshape.9), channel_id=1, replica_groups=mesh['query'=8,'space'=16] {'space'}, dimensions={0}, use_global_device_ids=true | all-gather | bytes 278528 | tf_op jit(solution)/shard_map/all_gather | solution.py:17
  254.5 23.9 %all-gather.5.cloned.1.call-done = f32[16,512,256]{2,1,0:T(8,128)} async-done(((f32[1,512,256]{2,1,0:T(8,128)}), f32[16,512,256]{2,1,0:T(8,128)}) %all-gather.5.cloned.1.call-update) | async-done | bytes 8388624 | tf_op jit(solution)/shard_map/all_gather | solution.py:17
  279.7 23.7 %while.34 = (s32[]{:T(128)}, f32[512,8]{0,1:T(8,128)S(1)}, f32[512,8]{0,1:T(8,128)S(1)}, f32[512,256]{0,1:T(8,128)S(1)}, f32[16,512,8]{1,2,0:T(8,128)S(1)}, /*in...) while((s32[]{:T(128)}, f32[512,8]{0,1:T(8,128)S(1)}, ...), condition=%wide.region_6.7_spmd, body=%wide.region_5.6_spmd.sunk | while | flops 417797 | bytes 3834007 | solution.py:22
  304.8 9.8 %convolution_multiply_fusion = f32[512,8192]{1,0:T(8,128)} fusion(bf16[8192,256]{1,0:T(8,128)(2,1)} %all-gather.3.cloned.1.call-done, bf16[512,256]{0,1:T(8,128)(2,1)S(1)} %multiply_convert_fusion, bf16[256,256]{1,0:T(8,128)(2,1)S(1)} %copy-done), kind=kOutput, calls=%fused_computation.36 | convolution fusion | flops 2218917888 | bytes 21364736 | tf_op jit(solution)/shard_map/qd,sd->qs/dot_general | solution.py:112
  (233 shorter events, 113.7 us)
Async XLA Ops:
  7.2 297.7 %copy-start = (bf16[256,256]{1,0:T(8,128)(2,1)S(1)}, bf16[256,256]{1,0:T(8,128)(2,1)}, u32[]{:S(2)}) copy-start(bf16[256,256]{1,0:T(8,128)(2,1)} %param.21) | copy-start | bytes 393220
  7.2 7.1 %copy-start.2 = (bf16[512,256]{1,0:T(8,128)(2,1)S(1)}, bf16[512,256]{1,0:T(8,128)(2,1)}, u32[]{:S(2)}) copy-start(bf16[512,256]{1,0:T(8,128)(2,1)} %param.13) | copy-start | bytes 786436
  7.2 7.1 %copy-start.5 = (bf16[256,256]{1,0:T(8,128)(2,1)S(1)}, bf16[256,256]{1,0:T(8,128)(2,1)}, u32[]{:S(2)}) copy-start(bf16[256,256]{1,0:T(8,128)(2,1)} %param.16) | copy-start | bytes 393220
  7.2 37.2 %all-gather.3.cloned.1.call-start = ((), (), s32[]{:S(2)}) async-start(), calls=%async_computation | async-start | bytes 4718592 | tf_op jit(solution)/shard_map/all_gather | solution.py:59
  7.9 270.5 %all-gather.5.cloned.1.call-start = ((), (), s32[]{:S(2)}) async-start(), calls=%async_computation.1 | async-start | bytes 8912896 | tf_op jit(solution)/shard_map/all_gather | solution.py:17
  10.9 33.5 %copy-start.3 = (bf16[256,256]{1,0:T(8,128)(2,1)S(1)}, bf16[256,256]{1,0:T(8,128)(2,1)}, u32[]{:S(2)}) copy-start(bf16[256,256]{1,0:T(8,128)(2,1)} %param.17) | copy-start | bytes 393220
  15.0 35.0 %copy-start.4 = (bf16[256,256]{1,0:T(8,128)(2,1)S(1)}, bf16[256,256]{1,0:T(8,128)(2,1)}, u32[]{:S(2)}) copy-start(bf16[256,256]{1,0:T(8,128)(2,1)} %param.18) | copy-start | bytes 393220
  44.4 5.6 %copy-start.1 = (bf16[8192,256]{1,0:T(8,128)(2,1)S(1)}, bf16[8192,256]{1,0:T(8,128)(2,1)}, u32[]{:S(2)}) copy-start(bf16[8192,256]{1,0:T(8,128)(2,1)} %all-gather.3.cloned.1.call-done) | copy-start | bytes 12582916
  279.7 23.7 %copy-start.6 = (bf16[256,256]{1,0:T(8,128)(2,1)S(1)}, bf16[256,256]{1,0:T(8,128)(2,1)}, u32[]{:S(2)}) copy-start(bf16[256,256]{1,0:T(8,128)(2,1)} %param.19) | copy-start | bytes 393220
  279.7 24.1 %copy-start.7 = (f32[256]{0:T(256)S(1)}, f32[256]{0:T(256)}, u32[]{:S(2)}) copy-start(f32[256]{0:T(256)} %param.20) | copy-start | bytes 3076
Sparse Core Ops, SparseCore 0:
  9.7 34.5 all-gather.2
  206.4 72.0 all-gather.4
where the time goes:
time: 324 us; the launch traced here: 321 us
  local copies, waits for them, and re-layouts  103 us (32%)
  matrix products  67.8 us (21%)
  waiting for transfers between devices  54 us (17%)
  blocking collectives  47.9 us (15%)
  other arithmetic  33.2 us (10%)
  between operations  14.3 us (4%)
    all_gather x2, blocking collectives, merged(): gathered = jax.tree.map(lambda a: lax.all_gather(a, axis), part)  47.9 us
    gather x16, local copies, waits for them, and re-layouts, block_partials(): picked_keys = key_blocks[chosen].reshape(-1, H, HD)  31.1 us
    gather x16, local copies, waits for them, and re-layouts, block_partials(): picked_values = value_blocks[chosen].reshape(-1, H, HD)  31 us
    all_gather x1, waiting for transfers between devices, shards(): whole_features = lax.all_gather(features, 'query', axis=0, tiled=True)  29.4 us
    reduce_sum x8, other arithmetic, block_partials(): block_totals = jnp.sum(numerators, axis=-1)  26.3 us
    dot_general x8, matrix products, block_partials(): jnp.einsum('hqk,khd->qhd', numerators.astype(jnp.bfloat16), picked_values...  26.1 us
    all_gather x1, waiting for transfers between devices, merged(): gathered = jax.tree.map(lambda a: lax.all_gather(a, axis), part)  23.9 us
    dot_general x8, matrix products, block_partials(): jnp.einsum('qhd,khd->hqk', heads, picked_keys, preferred_element_type=jnp...  22.7 us
  transfers between devices with their start and end apart: 2, of which 2 were waited for; matrix products, arithmetic and copies ran while one was open for 2% of the time, Pallas kernels for 0%

commit v1 on v0

v1 whole, which is shorter than its diff:
```python
import functools
import math

import jax
import jax.numpy as jnp
from jax import lax
from jax.experimental import pallas as pl
from jax.experimental.pallas import tpu as pltpu
from jax.sharding import PartitionSpec as P

D = 256
H = 8
HD = 32
QBLK = 64
SBLK = 128
CAP = 16
LOG2E = math.log2(math.e)
BF16 = jnp.bfloat16
F32 = jnp.float32
NT = (((1,), (1,)), ((), ()))
TN = (((0,), (0,)), ((), ()))
TAIL = 128
CHIPS = 4
OWN_BLOCKS = 8
SHARD_BLOCKS = 2 * CHIPS * OWN_BLOCKS
PHASES = 3
WIDTH = 20
COUNTS = PHASES * WIDTH
PAIRS = H // 2
WIDE = 2 * QBLK
MIB = 1024 * 1024
IN_SMEM = pl.BlockSpec(memory_space=pltpu.SMEM)
IN_VMEM = pl.BlockSpec(memory_space=pltpu.VMEM)
IN_HBM = pl.BlockSpec(memory_space=pltpu.HBM)


def head_of_lane(shape):
    return lax.broadcasted_iota(jnp.int32, shape, len(shape) - 1) // HD


def local_lists(place_ref, lists):
    chip, core = lax.div(place_ref[0], 2), lax.rem(place_ref[0], 2)
    inside = lax.rem(lists, OWN_BLOCKS)
    device = lax.rem(lax.div(lists, OWN_BLOCKS), 2 * CHIPS)
    other = jnp.where(lax.rem(device, 2) == core, 0, 1)
    ahead = lax.rem(lax.div(device, 2) - chip + CHIPS, CHIPS)
    near = jnp.where(ahead == 1, 2, 0) * OWN_BLOCKS + other * OWN_BLOCKS + inside
    half = OWN_BLOCKS // 2
    far = lax.div(inside, half) * OWN_BLOCKS + other * half + lax.rem(inside, half)
    position = jnp.where(ahead == 2, far, near)
    phase = jnp.where(ahead == 0, 0, jnp.where(ahead == 2, 2, 1))
    phase = jnp.where(lax.div(lists, SHARD_BLOCKS) == place_ref[1], phase, -1)
    width = lists.shape[0]
    row = lax.broadcasted_iota(jnp.int32, (width, width), 0)
    column = lax.broadcasted_iota(jnp.int32, (width, width), 1)
    earlier = jnp.where(column < row, 1.0, 0.0).astype(BF16)
    code = jnp.full(lists.shape, -1.0, F32)
    for p in range(PHASES):
        mine = phase == p
        rank = jnp.dot(earlier, jnp.where(mine, 1.0, 0.0).astype(BF16), preferred_element_type=F32)
        code = jnp.where(mine, (p * WIDTH + rank) * 128.0 + position.astype(F32), code)
    return code


def project_kernel(place_ref, lists_ref, queries_ref, wq_ref, wk_ref, out_ref, ids_ref, lists, queries, wq, wk, ids, sems):
    blocks = out_ref.shape[0]
    copies = [
        pltpu.make_async_copy(source, target, sems.at[i])
        for i, (source, target) in enumerate(
            [(lists_ref, lists), (queries_ref, queries), (wq_ref, wq), (wk_ref, wk)]
        )
    ]
    for copy in copies:
        copy.start()
    copies[0].wait()
    code = local_lists(place_ref, lists[...])
    list_row = lax.broadcasted_iota(jnp.int32, code.shape, 1)
    lane = lax.broadcasted_iota(jnp.int32, (code.shape[0], 128), 1)
    for b in range(blocks):
        wanted = place_ref[0] * blocks + b
        mine = jnp.sum(jnp.where(list_row == wanted, code, 0.0), axis=1, keepdims=True).astype(jnp.int32)
        slot = jnp.where(mine < 0, -1, lax.div(mine, 128))
        found = jnp.where(slot == lane, lax.rem(mine, 128), 0)
        phase = jnp.where(slot < 0, -1, lax.div(slot, WIDTH))
        found = found + jnp.where(phase == lane - COUNTS, jnp.where(phase < 0, 0, 1), 0)
        ids[b : b + 1, :] = jnp.sum(found.astype(F32), axis=0, keepdims=True).astype(jnp.int32)
    tell = pltpu.make_async_copy(ids, ids_ref, sems.at[4])
    tell.start()
    for copy in copies[1:]:
        copy.wait()
    proj = jnp.dot(queries[...], wq[...], preferred_element_type=F32).astype(BF16)
    head = head_of_lane((QBLK, D))
    scale = LOG2E / math.sqrt(HD)
    none = jnp.zeros((QBLK, D), BF16)
    for b in range(blocks):
        rows = proj[b * QBLK : (b + 1) * QBLK]
        for c in range(PAIRS):
            two = [jnp.where(head == h, rows, none) for h in (2 * c, 2 * c + 1)]
            folded = lax.dot_general(wk[...], jnp.concatenate(two, axis=0), NT, preferred_element_type=F32)
            out_ref[b, :, c * WIDE : (c + 1) * WIDE] = (folded * scale).astype(BF16)
    tell.wait()


def project(place, lists, queries, w_query, w_key):
    blocks = queries.shape[0] // QBLK
    return pl.pallas_call(
        project_kernel,
        out_shape=(
            jax.ShapeDtypeStruct((blocks, D, H * QBLK), BF16),
            jax.ShapeDtypeStruct((blocks, 128), jnp.int32),
        ),
        in_specs=[IN_SMEM] + [IN_HBM] * 4,
        out_specs=(IN_VMEM, IN_SMEM),
        scratch_shapes=[
            pltpu.VMEM(lists.shape, jnp.int32),
            pltpu.VMEM(queries.shape, BF16),
            pltpu.VMEM((D, D), BF16),
            pltpu.VMEM((D, D), BF16),
            pltpu.VMEM((blocks, 128), jnp.int32),
            pltpu.SemaphoreType.DMA((5,)),
        ],
        compiler_params=pltpu.CompilerParams(vmem_limit_bytes=16 * MIB),
        cost_estimate=pl.CostEstimate(
            flops=2 * queries.shape[0] * D * D * (H + 1), bytes_accessed=3 * MIB, transcendentals=0
        ),
        name="project",
    )(place, lists, queries, w_query, w_key)


def score(item, items, feats, q_ref, scores):
    keys = [feats[pl.ds(pl.multiple_of(items[item, 1 + k], SBLK), SBLK), :] for k in range(2)]
    scores[...] = jnp.dot(jnp.concatenate(keys, axis=0), q_ref[items[item, 3]], preferred_element_type=F32)


def weigh(item, items, feats, scores, acc, stats):
    b = items[item, 0]
    keys = [feats[pl.ds(pl.multiple_of(items[item, 1 + k], SBLK), SBLK), :] for k in range(2)]
    turned = jnp.concatenate(keys, axis=0).T
    alone = items[item, 4] == 1
    halves = H * QBLK // 2
    for c in range(2):
        part = slice(c * halves, (c + 1) * halves)
        first = scores[:SBLK, part]
        second = jnp.where(alone, -jnp.inf, scores[SBLK:, part])
        top = stats[b, 0:1, part]
        higher = jnp.maximum(top, jnp.max(jnp.maximum(first, second), axis=0, keepdims=True))
        factor = jnp.exp2(top - higher)
        first = jnp.exp2(first - higher)
        second = jnp.exp2(second - higher)
        stats[b, 0:1, part] = higher
        stats[b, 1:2, part] = stats[b, 1:2, part] * factor + jnp.sum(first + second, axis=0, keepdims=True)
        weights = jnp.concatenate([first.astype(BF16), second.astype(BF16)], axis=0)
        acc[b, :, part] = acc[b, :, part] * factor + jnp.dot(turned, weights, preferred_element_type=F32)


def attend_kernel(phase, sizes, last, ids_ref, q_ref, *rest):
    count = len(sizes)
    piece_refs, rest = rest[:count], rest[count:]
    if phase:
        rest = rest[2:]
    if last:
        wv_ref, rest = rest[0], rest[1:]
        acc, stats_ref, out_ref, feats, items, even, odd, wv, sems = rest
        load = pltpu.make_async_copy(wv_ref, wv, sems.at[0])
        load.start()
    else:
        acc, stats_ref, feats, items, even, odd, sems = rest
    held = 0
    for i, (size, ref) in enumerate(zip(sizes, piece_refs)):
        if phase == 0 and i == 0:
            own = pltpu.make_async_copy(ref, feats.at[pl.ds(held, size)], sems.at[1])
            own.start()
        else:
            feats[held : held + size, :] = ref[...]
        held += size
    blocks = q_ref.shape[0]

    def put(at, b, first, second, query, alone):
        for k, value in enumerate((b, first, second, query, alone)):
            items[at, k] = value

    def one_block(b, held):
        found = ids_ref[b, COUNTS + phase]

        def one(i, held):
            first = ids_ref[b, phase * WIDTH + 2 * i] * SBLK
            alone = 2 * i + 1 >= found
            second = jnp.where(alone, first, ids_ref[b, phase * WIDTH + 2 * i + 1] * SBLK)
            put(held, b, first, second, b, jnp.where(alone, 1, 0))
            return held + 1

        return lax.fori_loop(0, lax.div(found + 1, 2), one, held)

    total_items = lax.fori_loop(0, blocks, one_block, 0)
    for k in range(2):
        put(total_items + k, blocks, 0, 0, 0, 0)
    if phase == 0:
        acc[...] = jnp.zeros(acc.shape, F32)
        stats_ref[:, 0:1, :] = jnp.full((acc.shape[0], 1, H * QBLK), -jnp.inf, F32)
        stats_ref[:, 1:2, :] = jnp.zeros((acc.shape[0], 1, H * QBLK), F32)
        own.wait()
    score(0, items, feats, q_ref, even)

    def two_items(i, carry):
        score(2 * i + 1, items, feats, q_ref, odd)
        weigh(2 * i, items, feats, even, acc, stats_ref)
        score(2 * i + 2, items, feats, q_ref, even)
        weigh(2 * i + 1, items, feats, odd, acc, stats_ref)
        return carry

    lax.fori_loop(0, lax.div(total_items + 1, 2), two_items, 0)
    if not last:
        return
    load.wait()
    wv_t = wv[...].T
    slot = lax.broadcasted_iota(jnp.int32, (16, WIDE), 0)
    column = lax.broadcasted_iota(jnp.int32, (QBLK, D + TAIL), 1)
    odd_head = jnp.where(column < D, lax.rem(lax.div(column, HD), 2), lax.rem(lax.div(column, 16), 2))
    empty = jnp.zeros((TAIL - 32, WIDE), F32)
    for b in range(q_ref.shape[0]):
        diagonal = []
        tail = jnp.zeros((16, WIDE), F32)
        for c in range(PAIRS):
            part = slice(c * WIDE, (c + 1) * WIDE)
            total = stats_ref[b, 1:2, part]
            mean = (acc[b, :, part] * (1.0 / total)).astype(BF16)
            heads = slice(2 * HD * c, 2 * HD * (c + 1))
            diagonal.append(jnp.dot(wv_t[heads], mean, preferred_element_type=F32))
            level = stats_ref[b, 0:1, part] + jnp.log(total) * LOG2E
            for piece in range(3):
                rounded = level.astype(BF16).astype(F32)
                level = level - rounded
                tail = jnp.where(slot == piece * PAIRS + c, rounded, tail)
        turned = jnp.concatenate(diagonal + [tail, tail, empty], axis=0).T
        rows = jnp.where(odd_head == 1, turned[QBLK:], turned[:QBLK])
        out_ref[b * QBLK : (b + 1) * QBLK, :] = rows.astype(BF16)


def attend(phase, ids, folded, arrays, state, w_value):
    blocks = folded.shape[0]
    last = w_value is not None
    sizes = [a.shape[0] for a in arrays]
    out_shape = [
        jax.ShapeDtypeStruct((blocks + 1, D, H * QBLK), F32),
        jax.ShapeDtypeStruct((blocks + 1, 8, H * QBLK), F32),
    ]
    args = [ids, folded, *arrays]
    in_specs = [IN_SMEM, IN_VMEM] + [IN_VMEM] * len(arrays)
    most = blocks * (CAP // 2 + 1) + 2
    scratch = [pltpu.VMEM((sum(sizes), D), BF16), pltpu.SMEM((most, 8), jnp.int32)]
    scratch += [pltpu.VMEM((2 * SBLK, H * QBLK), F32)] * 2
    aliases = {}
    if phase == 0:
        in_specs[2] = IN_HBM
    else:
        aliases = {len(args): 0, len(args) + 1: 1}
        args += list(state)
        in_specs += [IN_VMEM] * 2
    if last:
        args.append(w_value)
        in_specs.append(IN_HBM)
        out_shape.append(jax.ShapeDtypeStruct((blocks * QBLK, D + TAIL), BF16))
        scratch.append(pltpu.VMEM((D, D), BF16))
    return pl.pallas_call(
        functools.partial(attend_kernel, phase, sizes, last),
        out_shape=out_shape,
        in_specs=in_specs,
        out_specs=[IN_VMEM] * len(out_shape),
        input_output_aliases=aliases,
        scratch_shapes=scratch + [pltpu.SemaphoreType.DMA((2,))],
        compiler_params=pltpu.CompilerParams(vmem_limit_bytes=16 * MIB),
        cost_estimate=pl.CostEstimate(flops=1_000_000_000, bytes_accessed=4 * MIB, transcendentals=700_000),
        name="attend_%d" % phase,
    )(*args)


def finish_kernel(place_ref, got_ref, queries_ref, wo_ref, gain_ref, out_ref, queries, wo, gain, sems):
    sources, count, _ = got_ref.shape
    first = pl.multiple_of(place_ref[1] * count, count)
    copies = [
        pltpu.make_async_copy(queries_ref.at[pl.ds(first, count)], queries, sems.at[0]),
        pltpu.make_async_copy(wo_ref, wo, sems.at[1]),
        pltpu.make_async_copy(gain_ref, gain, sems.at[2]),
    ]
    for copy in copies:
        copy.start()
    slot = lax.broadcasted_iota(jnp.int32, (TAIL, D), 0)
    pairs = H // 2
    head = 2 * lax.rem(slot, pairs) + lax.div(slot, 16)
    spread = (head == head_of_lane((TAIL, D))) & (lax.rem(slot, 16) < 3 * pairs) & (slot < 32)
    spread = jnp.where(spread, 1.0, 0.0).astype(BF16)
    tails = got_ref[:, :, D:].reshape(sources * count, TAIL)
    levels = jnp.dot(tails, spread, preferred_element_type=F32).reshape(sources, count, D)
    factors = jnp.exp2(levels - jnp.max(levels, axis=0, keepdims=True))
    mixed = jnp.sum(factors * got_ref[:, :, :D].astype(F32), axis=0)
    attended = (mixed / jnp.sum(factors, axis=0)).astype(BF16)
    for copy in copies:
        copy.wait()
    rows = queries[...].astype(F32) + jnp.dot(attended, wo[...], preferred_element_type=F32)
    center = rows - jnp.mean(rows, axis=1, keepdims=True)
    variance = jnp.mean(center * center, axis=1, keepdims=True)
    updated = (center * lax.rsqrt(variance + 1e-05) * gain[...]).astype(BF16)
    for i in range(sources):
        out_ref[i] = updated


def finish(place, got, queries, w_out, norm_gain):
    sources, count, _ = got.shape
    return pl.pallas_call(
        finish_kernel,
        out_shape=jax.ShapeDtypeStruct((sources, count, D), BF16),
        in_specs=[IN_SMEM, IN_VMEM] + [IN_HBM] * 3,
        out_specs=IN_VMEM,
        scratch_shapes=[
            pltpu.VMEM((count, D), BF16),
            pltpu.VMEM((D, D), BF16),
            pltpu.VMEM((1, D), F32),
            pltpu.SemaphoreType.DMA((3,)),
        ],
        compiler_params=pltpu.CompilerParams(vmem_limit_bytes=16 * MIB),
        cost_estimate=pl.CostEstimate(flops=10_000_000, bytes_accessed=MIB, transcendentals=140_000),
        name="finish",
    )(place, got, queries, w_out, norm_gain.reshape(1, D))


STEP = 512
SLOTS = 4


def piece_row(place_ref, piece):
    ahead, other, row = piece
    index = place_ref[0]
    chip = lax.rem(lax.div(index, 2) + ahead + CHIPS, CHIPS)
    core = lax.rem(index, 2)
    core = 1 - core if other else core
    return (chip * 2 + core) * (OWN_BLOCKS * SBLK) + row


def logits_kernel(pieces, place_ref, updated_ref, wm_ref, own_ref, *rest):
    count = len(pieces)
    piece_refs = rest[: count - 1]
    updated_out, out_ref, embed, wm, own, tiles, in_sems, out_sems = rest[count - 1 :]
    load_wm = pltpu.make_async_copy(wm_ref, wm, in_sems.at[0])
    load_wm.start()
    load_own = pltpu.make_async_copy(own_ref, own, in_sems.at[1])
    load_own.start()
    keep = pltpu.make_async_copy(updated_ref, updated_out, in_sems.at[2])
    keep.start()
    load_wm.wait()
    rows = jnp.dot(updated_ref[...], wm[...], preferred_element_type=F32).astype(BF16)
    embed[...] = rows * (1.0 / math.sqrt(D))
    stores = []
    for i, ref in [*enumerate(piece_refs, 1), (0, own)]:
        if i == 0:
            load_own.wait()
        for row in range(0, ref.shape[0], STEP):
            slot = len(stores) % SLOTS
            if len(stores) >= SLOTS:
                stores[-SLOTS].wait()
            tiles[slot] = lax.dot_general(
                embed[...], ref[row : row + STEP, :], NT, preferred_element_type=F32
            )
            column = pl.multiple_of(piece_row(place_ref, pieces[i]) + row, STEP)
            stores.append(
                pltpu.make_async_copy(tiles.at[slot], out_ref.at[:, pl.ds(column, STEP)], out_sems.at[slot])
            )
            stores[-1].start()
    for store in stores[-SLOTS:]:
        store.wait()
    keep.wait()


def logits(place, updated, w_mask, pieces, arrays):
    count = updated.shape[0]
    shard = sum(a.shape[0] for a in arrays)
    return pl.pallas_call(
        functools.partial(logits_kernel, pieces),
        out_shape=(
            jax.ShapeDtypeStruct(updated.shape, BF16),
            jax.ShapeDtypeStruct((count, shard), F32),
        ),
        in_specs=[IN_SMEM, IN_VMEM, IN_HBM, IN_HBM] + [IN_VMEM] * (len(arrays) - 1),
        out_specs=(IN_HBM, IN_HBM),
        scratch_shapes=[
            pltpu.VMEM((count, D), BF16),
            pltpu.VMEM((D, D), BF16),
            pltpu.VMEM(arrays[0].shape, BF16),
            pltpu.VMEM((SLOTS, count, STEP), F32),
            pltpu.SemaphoreType.DMA((3,)),
            pltpu.SemaphoreType.DMA((SLOTS,)),
        ],
        compiler_params=pltpu.CompilerParams(vmem_limit_bytes=16 * MIB),
        cost_estimate=pl.CostEstimate(
            flops=2 * count * shard * D, bytes_accessed=20 * MIB, transcendentals=0
        ),
        name="logits",
    )(place, updated, w_mask, *arrays)


def shards(queries, features, block_lists, w_query, w_key, w_value, w_out, norm_gain, w_mask):
    space = lax.axis_size("space")
    place = jnp.stack([lax.axis_index("query"), lax.axis_index("space")]).astype(jnp.int32)
    up = [(y * 2 + c, (y + 1) % CHIPS * 2 + c) for y in range(CHIPS) for c in range(2)]
    down = [(y * 2 + c, (y - 1) % CHIPS * 2 + c) for y in range(CHIPS) for c in range(2)]
    cores = [(i, i ^ 1) for i in range(2 * CHIPS)]

    def send(rows, pairs):
        return lax.ppermute(rows, "query", pairs)

    below = send(features, up)
    above = send(features, down)
    beside = send(features, cores)
    folded, ids = project(place, block_lists.T, queries, w_query, w_key)
    state = attend(0, ids, folded, [features, beside], None, None)
    below, above, state = lax.optimization_barrier((below, above, tuple(state)))
    half = features.shape[0] // 2
    far_low = send(below[:half], up)
    far_high = send(above[half:], down)
    near = [below, send(below, cores), above, send(above, cores)]
    state = attend(1, ids, folded, near, state, None)
    far_low, far_high, state = lax.optimization_barrier((far_low, far_high, tuple(state)))
    far = [far_low, send(far_low, cores), far_high, send(far_high, cores)]
    partial = attend(2, ids, folded, far, state, w_value)[2]

    count = queries.shape[0] // space
    got = lax.all_to_all(partial.reshape(space, count, D + TAIL), "space", 0, 0)
    mine = finish(place, got, queries, w_out, norm_gain)
    updated = lax.all_to_all(mine, "space", 0, 0).reshape(queries.shape)
    pieces = [(0, False, 0), (0, True, 0), (-1, False, 0), (-1, True, 0), (1, False, 0), (1, True, 0)]
    pieces += [(-2, False, 0), (-2, True, 0), (2, False, half), (2, True, half)]
    return logits(place, updated, w_mask, pieces, [features, beside, *near, *far])


def solution(mesh):
    placed = (P("query", None), P(("space", "query"), None), P(), P(), P(), P(), P(), P(), P())
    return jax.shard_map(
        shards,
        mesh=mesh,
        in_specs=placed,
        out_specs=(P("query", None), P("query", "space")),
        check_vma=False,
    )
```

time: 324 us -> 73.7 us (0.23)
  local copies, waits for them, and re-layouts: 103 us -> 4.6 us
  matrix products: 67.8 us -> 0 us
  waiting for transfers between devices: 54 us -> 7.25 us
  other arithmetic: 33.2 us -> 0.07 us
  Pallas kernels: 0 us -> 25.5 us
  blocking collectives: 47.9 us -> 29.1 us
  between operations: 14.3 us -> 0.76 us
  starting transfers between devices: 0.08 us -> 6.37 us
    dot_general x21 -> x0, matrix products: 67.8 us -> none  [the longest x8 26.1 us: block_partials(): jnp.einsum('hqk,khd->qhd', numerators.astype(jnp.bfloat16), picked_values...]
    gather x40 -> x0, local copies, waits for them, and re-layouts: 65.4 us -> none  [the longest x16 31.1 us: block_partials(): picked_keys = key_blocks[chosen].reshape(-1, H, HD)]
    all_gather x2 -> x0, waiting for transfers between devices: 53.3 us -> none  [the longest x1 29.4 us: shards(): whole_features = lax.all_gather(features, 'query', axis=0, tiled=True)]
    all_gather x2 -> x0, blocking collectives: 47.9 us -> none  [merged(): gathered = jax.tree.map(lambda a: lax.all_gather(a, axis), part)]
    all_to_all x0 -> x2, blocking collectives: none -> 29.1 us  [the longest x1 17.1 us: shards(): got = lax.all_to_all(partial.reshape(space, count, D + TAIL), 'space', 0, 0)]
    reduce_sum x9 -> x0, other arithmetic: 26.4 us -> none  [the longest x8 26.3 us: block_partials(): block_totals = jnp.sum(numerators, axis=-1)]
    pallas_call x0 -> x6, Pallas kernels: none -> 25.5 us  [the longest x3 13.3 us: attend(): pl.pallas_call(functools.partial(attend_kernel, phase, sizes, last), out_...]
    dynamic_slice x30 -> x0, local copies, waits for them, and re-layouts: 19.2 us -> none  [take(): lax.dynamic_index_in_dim(a, source, 0, False)]
  transfers between devices with their start and end apart: 2 -> 9, of which waited for: 2 -> 6; matrix products, arithmetic and copies ran while one was open for 2% -> 0% of each run, Pallas kernels for 0% -> 17%
where the time goes in v1:
time: 73.7 us
  blocking collectives  29.1 us (39%)
  Pallas kernels  25.5 us (35%)
  waiting for transfers between devices  7.25 us (10%)
  starting transfers between devices  6.37 us (9%)
  local copies, waits for them, and re-layouts  4.6 us (6%)
  between operations  0.76 us (1%)
    all_to_all x1, blocking collectives, shards(): got = lax.all_to_all(partial.reshape(space, count, D + TAIL), 'space', 0, 0)  17.1 us
    pallas_call x3, Pallas kernels, attend(): pl.pallas_call(functools.partial(attend_kernel, phase, sizes, last), out_...  13.3 us
    all_to_all x1, blocking collectives, shards(): updated = lax.all_to_all(mine, 'space', 0, 0).reshape(queries.shape)  12 us
    ppermute x9, waiting for transfers between devices, send(): return lax.ppermute(rows, 'query', pairs)  7.25 us
    pallas_call x1, Pallas kernels, logits(): pl.pallas_call(functools.partial(logits_kernel, pieces), out_shape=(jax.S...  7.2 us
    ppermute x9, starting transfers between devices, send(): return lax.ppermute(rows, 'query', pairs)  6.37 us
    unnamed x22, local copies, waits for them, and re-layouts  4.56 us
    pallas_call x1, Pallas kernels, project(): pl.pallas_call(project_kernel, out_shape=(jax.ShapeDtypeStruct((blocks, D...  3.58 us
  transfers between devices with their start and end apart: 9, of which 6 were waited for; matrix products, arithmetic and copies ran while one was open for 0% of the time, Pallas kernels for 17%

profile of v1, /device:TPU:0, one launch (start us, length us, event | category | flops | bytes accessed | tf_op | source)
XLA Modules:
  0.0 73.7 jit_solution(15403950825973723753)
XLA Ops:
  0.6 0.1 collective-permute-start.2
  0.7 3.2 %collective-permute-start.1 = (bf16[1024,256]{1,0:T(8,128)(2,1)}, bf16[1024,256]{1,0:T(8,128)(2,1)S(1)}, u32[]{:S(2)}, u32[]{:S(2)}) collective-permute-start(bf16[1024,256]{1,0:T(8,128)(2,1)} %own_ref.1), channel_id=1, source_target_pairs={{0,96},{16,112},{32,0},{48,16},{64,32},{80,48},{96,64},{112,80},{1... | collective-permute-start | bytes 1572872 | tf_op jit(solution)/shard_map/ppermute | solution.py:408
  3.9 0.1 pad_add_fusion.place_ref
  4.0 0.9 %copy-done = bf16[512,256]{1,0:T(8,128)(2,1)S(1)} copy-done((bf16[512,256]{1,0:T(8,128)(2,1)S(1)}, bf16[512,256]{1,0:T(8,128)(2,1)}, u32[]{:S(2)}) %copy-start) | copy-done | bytes 262168
  4.9 0.9 %copy-done.7 = bf16[256,256]{1,0:T(8,128)(2,1)S(1)} copy-done((bf16[256,256]{1,0:T(8,128)(2,1)S(1)}, bf16[256,256]{1,0:T(8,128)(2,1)}, u32[]{:S(2)}) %copy-start.7) | copy-done | bytes 131096
  5.8 0.9 %copy-done.8 = bf16[256,256]{1,0:T(8,128)(2,1)S(1)} copy-done((bf16[256,256]{1,0:T(8,128)(2,1)S(1)}, bf16[256,256]{1,0:T(8,128)(2,1)}, u32[]{:S(2)}) %copy-start.8) | copy-done | bytes 131096
  6.7 0.7 copy-done.10
  7.5 3.6 %project.1 = (bf16[8,256,512]{2,1,0:T(8,128)(2,1)S(1)}, s32[8,128]{1,0:T(8,128)S(1)}) custom-call(s32[2]{0:T(128)S(1)} %pad_add_fusion.place_ref, s32[46,64]{1,0:T(8,128)S(1)} %bitcast.9, bf16[512,256]{1,0:T(8,128)(2,1)S(1)} %copy-done, bf16[256,256]{1,0:T(8,128)(2,1)S(1)} %copy-done.7, bf16[256,256]{1,0:T(8,128)(2,1)S(1)} %copy-done.8), custom_call_target="tpu_custom_call" | custom-call | flops 603979776 | bytes 3145728 | tf_op jit(solution)/shard_map/project/pallas_call | solution.py:106
  11.1 0.0 collective-permute-done.2.rest_1_.rest_0_
  11.1 0.0 copy-start.5
  11.1 1.0 %copy-done.5 = bf16[1024,256]{1,0:T(8,128)(2,1)S(1)} copy-done((bf16[1024,256]{1,0:T(8,128)(2,1)S(1)}, bf16[1024,256]{1,0:T(8,128)(2,1)}, u32[]{:S(2)}) %copy-start.5) | copy-done | bytes 524312
  12.1 3.2 %attend_0.1 = (f32[9,256,512]{2,1,0:T(8,128)S(1)}, f32[9,8,512]{2,1,0:T(8,128)S(1)}) custom-call(s32[8,128]{1,0:T(8,128)S(1)} %get-tuple-element.17.ids_ref, bf16[8,256,512]{2,1,0:T(8,128)(2,1)S(1)} %get-tuple-element.18.q_ref, bf16[1024,256]{1,0:T(8,128)(2,1)S(1)} %copy-done.5, bf16[1024,256]{1,0:T(8,128)(2,1)S(1)} %collective-permute-done.2.rest_1_.rest_0_), custom_call_target="tpu_custom_call" | custom-call | flops 1000000000 | bytes 4194304 | tf_op jit(solution)/shard_map/attend_0/pallas_call | solution.py:264
  15.4 0.6 collective-permute-done.1.rest_2_.rest_3_
  16.0 3.3 %collective-permute-done.rest_0_.rest_1_ = bf16[1024,256]{1,0:T(8,128)(2,1)S(1)} collective-permute-done((bf16[1024,256]{1,0:T(8,128)(2,1)}, bf16[1024,256]{1,0:T(8,128)(2,1)S(1)}, u32[]{:S(2)}, u32[]{:S(2)}) %collective-permute-start) | collective-permute-done | bytes 524320 | tf_op jit(solution)/shard_map/ppermute | solution.py:408
  19.3 0.5 collective-permute-start.6
  19.8 0.0 copy-start.2
  19.9 0.4 collective-permute-start.4
  20.2 1.7 %collective-permute-start.3 = (bf16[512,256]{1,0:T(8,128)(2,1)S(1)}, bf16[512,256]{1,0:T(8,128)(2,1)S(1)}, u32[]{:S(2)}, u32[]{:S(2)}) collective-permute-start(bf16[512,256]{1,0:T(8,128)(2,1)S(1)} %slice.6), channel_id=1, source_target_pairs={{0,32},{16,48},{32,64},{48,80},{64,96},{80,112},{96,0},{112,16},{1... | collective-permute-start | bytes 786440 | tf_op jit(solution)/shard_map/ppermute | solution.py:408
  22.0 5.5 %attend_1.1 = (f32[9,256,512]{2,1,0:T(8,128)S(1)}, f32[9,8,512]{2,1,0:T(8,128)S(1)}) custom-call(s32[8,128]{1,0:T(8,128)S(1)} %get-tuple-element.17.ids_ref, bf16[8,256,512]{2,1,0:T(8,128)(2,1)S(1)} %get-tuple-element.18.q_ref, bf16[1024,256]{1,0:T(8,128)(2,1)S(1)} %collective-permute-done.rest_0_.rest_1_, ...), custom_call_target="tpu_custom_call", output_to_operand_aliasing={{0}: (6, {}), {1}: (7, {})} | custom-call | flops 1000000000 | bytes 4194304 | tf_op jit(solution)/shard_map/attend_1/pallas_call | solution.py:264
  27.5 0.0 copy-start.1
  27.5 0.0 copy-start.3
  27.5 0.0 copy-start.4
  27.5 0.6 collective-permute-done.4.rest_2_.rest_7_
  28.2 1.3 %collective-permute-done.3.rest_0_.rest_5_ = bf16[512,256]{1,0:T(8,128)(2,1)S(1)} collective-permute-done((bf16[512,256]{1,0:T(8,128)(2,1)S(1)}, bf16[512,256]{1,0:T(8,128)(2,1)S(1)}, u32[]{:S(2)}, u32[]{:S(2)}) %collective-permute-start.3) | collective-permute-done | bytes 262176 | tf_op jit(solution)/shard_map/ppermute | solution.py:408
  29.5 0.5 collective-permute-start.8
  30.0 1.0 %collective-permute-done.7.rest_1_.rest_6_ = bf16[512,256]{1,0:T(8,128)(2,1)S(1)} collective-permute-done((bf16[512,256]{1,0:T(8,128)(2,1)S(1)}, bf16[512,256]{1,0:T(8,128)(2,1)S(1)}, u32[]{:S(2)}, u32[]{:S(2)}) %collective-permute-start.7) | collective-permute-done | bytes 262176 | tf_op jit(solution)/shard_map/ppermute | solution.py:408
  31.0 0.4 collective-permute-done.8.rest_3_.rest_8_
  31.4 4.5 %attend_2.1 = (f32[9,256,512]{2,1,0:T(8,128)S(1)}, f32[9,8,512]{2,1,0:T(8,128)S(1)}, bf16[512,384]{1,0:T(8,128)(2,1)S(1)}) custom-call(s32[8,128]{1,0:T(8,128)S(1)} %get-tuple-element.17.ids_ref, bf16[8,256,512]{2,1,0:T(8,128)(2,1)S(1)} %get-tuple-element.18.q_ref, ...), custom_call_target="tpu_custom_call", output_to_operand_aliasing={{0}: (6, {}), {1}: (7, {})} | custom-call | flops 1000000000 | bytes 4194304 | tf_op jit(solution)/shard_map/attend_2/pallas_call | solution.py:264
  35.9 17.1 %all_to_all.10.got_ref = bf16[16,32,384]{2,1,0:T(8,128)(2,1)S(1)} all-to-all(bf16[16,32,384]{2,1,0:T(8,128)(2,1)S(1)} %bitcast.6), channel_id=1, replica_groups=mesh['query'=8,'space'=16] {'space'}, dimensions={0} | all-to-all | bytes 786432 | tf_op jit(solution)/shard_map/all_to_all | solution.py:426
  53.0 1.4 %finish.1 = bf16[16,32,256]{2,1,0:T(8,128)(2,1)S(1)} custom-call(s32[2]{0:T(128)S(1)} %pad_add_fusion.place_ref, bf16[16,32,384]{2,1,0:T(8,128)(2,1)S(1)} %all_to_all.10.got_ref, bf16[512,256]{1,0:T(8,128)(2,1)S(1)} %copy-done.1, bf16[256,256]{1,0:T(8,128)(2,1)S(1)} %copy-done.3, f32[1,256]{1,0:T(1,128)S(1)} %bitcast.8), custom_call_target="tpu_custom_call" | custom-call | flops 10000000 | bytes 1048576 | tf_op jit(solution)/shard_map/finish/pallas_call | solution.py:309
  54.5 12.0 %all_to_all.11 = bf16[16,32,256]{2,1,0:T(8,128)(2,1)S(1)} all-to-all(bf16[16,32,256]{2,1,0:T(8,128)(2,1)S(1)} %finish.1), channel_id=1, replica_groups=mesh['query'=8,'space'=16] {'space'}, dimensions={0} | all-to-all | bytes 524288 | tf_op jit(solution)/shard_map/all_to_all | solution.py:428
  66.5 7.2 %logits.1 = (bf16[512,256]{1,0:T(8,128)(2,1)}, f32[512,8192]{1,0:T(8,128)}) custom-call(s32[2]{0:T(128)S(1)} %pad_add_fusion.place_ref, bf16[512,256]{1,0:T(8,128)(2,1)S(1)} %bitcast.7, bf16[256,256]{1,0:T(8,128)(2,1)S(1)} %copy-done.9, bf16[1024,256]{1,0:T(8,128)(2,1)S(1)} %copy-done.6, bf16[1024,256]{1,0:T(8,128)(2,1)S(1)} %collective-permute-done.2.rest_1_.rest_0_, ...), custom_call_target="tpu_custom_call" | custom-call | flops 2147483648 | bytes 20971520 | tf_op jit(solution)/shard_map/logits/pallas_call | solution.py:376
  (19 shorter events, 0.1 us)
Async XLA Ops:
  0.6 10.4 %collective-permute-start.2 = (bf16[1024,256]{1,0:T(8,128)(2,1)}, bf16[1024,256]{1,0:T(8,128)(2,1)S(1)}, u32[]{:S(2)}, u32[]{:S(2)}) collective-permute-start(bf16[1024,256]{1,0:T(8,128)(2,1)} %own_ref.1), channel_id=1, source_target_pairs={{0,16},{16,0},{32,48},{48,32},{64,80},{80,64},{96,112},{112,96},{1... | collective-permute-start | bytes 1572872 | tf_op jit(solution)/shard_map/ppermute | solution.py:408
  0.7 15.3 %collective-permute-start.1 = (bf16[1024,256]{1,0:T(8,128)(2,1)}, bf16[1024,256]{1,0:T(8,128)(2,1)S(1)}, u32[]{:S(2)}, u32[]{:S(2)}) collective-permute-start(bf16[1024,256]{1,0:T(8,128)(2,1)} %own_ref.1), channel_id=1, source_target_pairs={{0,96},{16,112},{32,0},{48,16},{64,32},{80,48},{96,64},{112,80},{1... | collective-permute-start | bytes 1572872 | tf_op jit(solution)/shard_map/ppermute | solution.py:408
  3.9 15.4 %collective-permute-start = (bf16[1024,256]{1,0:T(8,128)(2,1)}, bf16[1024,256]{1,0:T(8,128)(2,1)S(1)}, u32[]{:S(2)}, u32[]{:S(2)}) collective-permute-start(bf16[1024,256]{1,0:T(8,128)(2,1)} %own_ref.1), channel_id=1, source_target_pairs={{0,32},{16,48},{32,64},{48,80},{64,96},{80,112},{96,0},{112,16},{1... | collective-permute-start | bytes 1572872 | tf_op jit(solution)/shard_map/ppermute | solution.py:408
  4.0 1.0 %copy-start = (bf16[512,256]{1,0:T(8,128)(2,1)S(1)}, bf16[512,256]{1,0:T(8,128)(2,1)}, u32[]{:S(2)}) copy-start(bf16[512,256]{1,0:T(8,128)(2,1)} %queries_ref.3) | copy-start | bytes 786436
  4.9 0.9 %copy-start.7 = (bf16[256,256]{1,0:T(8,128)(2,1)S(1)}, bf16[256,256]{1,0:T(8,128)(2,1)}, u32[]{:S(2)}) copy-start(bf16[256,256]{1,0:T(8,128)(2,1)} %wq_ref.1) | copy-start | bytes 393220
  5.8 0.9 %copy-start.8 = (bf16[256,256]{1,0:T(8,128)(2,1)S(1)}, bf16[256,256]{1,0:T(8,128)(2,1)}, u32[]{:S(2)}) copy-start(bf16[256,256]{1,0:T(8,128)(2,1)} %wk_ref.1) | copy-start | bytes 393220
  6.7 0.7 %copy-start.10 = (s32[64,46]{0,1:T(8,128)S(1)}, s32[64,46]{0,1:T(8,128)}, u32[]{:S(2)}) copy-start(s32[64,46]{0,1:T(8,128)} %param.11) | copy-start | bytes 35332
  11.1 1.0 %copy-start.5 = (bf16[1024,256]{1,0:T(8,128)(2,1)S(1)}, bf16[1024,256]{1,0:T(8,128)(2,1)}, u32[]{:S(2)}) copy-start(bf16[1024,256]{1,0:T(8,128)(2,1)} %own_ref.1) | copy-start | bytes 1572868
  19.3 2.7 %collective-permute-start.5 = (bf16[1024,256]{1,0:T(8,128)(2,1)S(1)}, bf16[1024,256]{1,0:T(8,128)(2,1)S(1)}, u32[]{:S(2)}, u32[]{:S(2)}) collective-permute-start(bf16[1024,256]{1,0:T(8,128)(2,1)S(1)} %collective-permute-done.rest_0_.rest_1_), channel_id=1, source_target_pairs={{0,16},{16,0},{32,48},{48,32},{64,80},{80,64},{96,112},{112,96},{1... | collective-permute-start | bytes 1572872 | tf_op jit(solution)/shard_map/ppermute | solution.py:408
  19.3 2.7 %collective-permute-start.6 = (bf16[1024,256]{1,0:T(8,128)(2,1)S(1)}, bf16[1024,256]{1,0:T(8,128)(2,1)S(1)}, u32[]{:S(2)}, u32[]{:S(2)}) collective-permute-start(bf16[1024,256]{1,0:T(8,128)(2,1)S(1)} %collective-permute-done.1.rest_2_.rest_3_), channel_id=1, source_target_pairs={{0,16},{16,0},{32,48},{48,32},{64,80},{80,64},{96,112},{112,96},{1... | collective-permute-start | bytes 1572872 | tf_op jit(solution)/shard_map/ppermute | solution.py:408
  19.8 11.5 %copy-start.2 = (bf16[256,256]{1,0:T(8,128)(2,1)S(1)}, bf16[256,256]{1,0:T(8,128)(2,1)}, u32[]{:S(2)}) copy-start(bf16[256,256]{1,0:T(8,128)(2,1)} %rest_6_.1) | copy-start | bytes 393220
  19.9 8.3 %collective-permute-start.4 = (bf16[512,256]{1,0:T(8,128)(2,1)S(1)}, bf16[512,256]{1,0:T(8,128)(2,1)S(1)}, u32[]{:S(2)}, u32[]{:S(2)}) collective-permute-start(bf16[512,256]{1,0:T(8,128)(2,1)S(1)} %slice.7), channel_id=1, source_target_pairs={{0,96},{16,112},{32,0},{48,16},{64,32},{80,48},{96,64},{112,80},{1... | collective-permute-start | bytes 786440 | tf_op jit(solution)/shard_map/ppermute | solution.py:408
  20.2 9.2 %collective-permute-start.3 = (bf16[512,256]{1,0:T(8,128)(2,1)S(1)}, bf16[512,256]{1,0:T(8,128)(2,1)S(1)}, u32[]{:S(2)}, u32[]{:S(2)}) collective-permute-start(bf16[512,256]{1,0:T(8,128)(2,1)S(1)} %slice.6), channel_id=1, source_target_pairs={{0,32},{16,48},{32,64},{48,80},{64,96},{80,112},{96,0},{112,16},{1... | collective-permute-start | bytes 786440 | tf_op jit(solution)/shard_map/ppermute | solution.py:408
  27.5 25.5 %copy-start.1 = (bf16[512,256]{1,0:T(8,128)(2,1)S(1)}, bf16[512,256]{1,0:T(8,128)(2,1)}, u32[]{:S(2)}) copy-start(bf16[512,256]{1,0:T(8,128)(2,1)} %queries_ref.3) | copy-start | bytes 786436
  27.5 25.5 %copy-start.3 = (bf16[256,256]{1,0:T(8,128)(2,1)S(1)}, bf16[256,256]{1,0:T(8,128)(2,1)}, u32[]{:S(2)}) copy-start(bf16[256,256]{1,0:T(8,128)(2,1)} %wo_ref.1) | copy-start | bytes 393220
  27.5 25.5 %copy-start.4 = (f32[256]{0:T(256)S(1)}, f32[256]{0:T(256)}, u32[]{:S(2)}) copy-start(f32[256]{0:T(256)} %param.16) | copy-start | bytes 3076
  29.4 37.0 %copy-start.6 = (bf16[1024,256]{1,0:T(8,128)(2,1)S(1)}, bf16[1024,256]{1,0:T(8,128)(2,1)}, u32[]{:S(2)}) copy-start(bf16[1024,256]{1,0:T(8,128)(2,1)} %own_ref.1) | copy-start | bytes 1572868
  29.5 37.0 %copy-start.9 = (bf16[256,256]{1,0:T(8,128)(2,1)S(1)}, bf16[256,256]{1,0:T(8,128)(2,1)}, u32[]{:S(2)}) copy-start(bf16[256,256]{1,0:T(8,128)(2,1)} %wm_ref.1) | copy-start | bytes 393220
  29.5 1.5 %collective-permute-start.7 = (bf16[512,256]{1,0:T(8,128)(2,1)S(1)}, bf16[512,256]{1,0:T(8,128)(2,1)S(1)}, u32[]{:S(2)}, u32[]{:S(2)}) collective-permute-start(bf16[512,256]{1,0:T(8,128)(2,1)S(1)} %collective-permute-done.3.rest_0_.rest_5_), channel_id=1, source_target_pairs={{0,16},{16,0},{32,48},{48,32},{64,80},{80,64},{96,112},{112,96},{1... | collective-permute-start | bytes 786440 | tf_op jit(solution)/shard_map/ppermute | solution.py:408
  29.5 1.9 %collective-permute-start.8 = (bf16[512,256]{1,0:T(8,128)(2,1)S(1)}, bf16[512,256]{1,0:T(8,128)(2,1)S(1)}, u32[]{:S(2)}, u32[]{:S(2)}) collective-permute-start(bf16[512,256]{1,0:T(8,128)(2,1)S(1)} %collective-permute-done.4.rest_2_.rest_7_), channel_id=1, source_target_pairs={{0,16},{16,0},{32,48},{48,32},{64,80},{80,64},{96,112},{112,96},{1... | collective-permute-start | bytes 786440 | tf_op jit(solution)/shard_map/ppermute | solution.py:408

commit v2 on v1

v2 whole, which is shorter than its diff:
```python
import functools
import math

import jax
import jax.numpy as jnp
from jax import lax
from jax.experimental import pallas as pl
from jax.experimental.pallas import tpu as pltpu
from jax.sharding import PartitionSpec as P

D = 256
H = 8
HD = 32
QBLK = 64
SBLK = 128
CAP = 16
LOG2E = math.log2(math.e)
BF16 = jnp.bfloat16
F32 = jnp.float32
NT = (((1,), (1,)), ((), ()))
TN = (((0,), (0,)), ((), ()))
TAIL = 128
CHIPS = 4
OWN_BLOCKS = 8
SHARD_BLOCKS = 2 * CHIPS * OWN_BLOCKS
PHASES = 3
WIDTH = 20
LAST = 127
COUNTS = PHASES * WIDTH
PAIRS = H // 2
WIDE = 2 * QBLK
MIB = 1024 * 1024
IN_SMEM = pl.BlockSpec(memory_space=pltpu.SMEM)
IN_VMEM = pl.BlockSpec(memory_space=pltpu.VMEM)
IN_HBM = pl.BlockSpec(memory_space=pltpu.HBM)


def stay(array):
    return pltpu.with_memory_space_constraint(array, pltpu.HBM)


def head_of_lane(shape):
    return lax.broadcasted_iota(jnp.int32, shape, len(shape) - 1) // HD


def local_lists(place_ref, lists):
    chip, core = lax.div(place_ref[0], 2), lax.rem(place_ref[0], 2)
    inside = lax.rem(lists, OWN_BLOCKS)
    device = lax.rem(lax.div(lists, OWN_BLOCKS), 2 * CHIPS)
    other = jnp.where(lax.rem(device, 2) == core, 0, 1)
    ahead = lax.rem(lax.div(device, 2) - chip + CHIPS, CHIPS)
    near = jnp.where(ahead == 1, 2, 0) * OWN_BLOCKS + other * OWN_BLOCKS + inside
    half = OWN_BLOCKS // 2
    far = lax.div(inside, half) * OWN_BLOCKS + other * half + lax.rem(inside, half)
    position = jnp.where(ahead == 2, far, near)
    phase = jnp.where(ahead == 0, 0, jnp.where(ahead == 2, 2, 1))
    phase = jnp.where(lax.div(lists, SHARD_BLOCKS) == place_ref[1], phase, -1)
    width = lists.shape[0]
    row = lax.broadcasted_iota(jnp.int32, (width, width), 0)
    column = lax.broadcasted_iota(jnp.int32, (width, width), 1)
    earlier = jnp.where(column < row, 1.0, 0.0).astype(BF16)
    code = jnp.full(lists.shape, -1.0, F32)
    for p in range(PHASES):
        mine = phase == p
        rank = jnp.dot(earlier, jnp.where(mine, 1.0, 0.0).astype(BF16), preferred_element_type=F32)
        code = jnp.where(mine, (p * WIDTH + rank) * 128.0 + position.astype(F32), code)
    return code


def write_items(ids, items, blocks):
    for phase in range(PHASES):

        def one_block(b, held):
            found = ids[b, COUNTS + phase]

            def one(i, held):
                first = ids[b, phase * WIDTH + 2 * i]
                alone = 2 * i + 1 >= found
                second = jnp.where(alone, first, ids[b, phase * WIDTH + 2 * i + 1])
                items[phase, held] = ((jnp.where(alone, 1, 0) * 64 + second) * 64 + first) * 16 + b
                return held + 1

            return lax.fori_loop(0, lax.div(found + 1, 2), one, held)

        total = lax.fori_loop(0, blocks, one_block, 0)
        items[phase, total] = blocks
        items[phase, total + 1] = blocks
        items[phase, LAST] = total


def project_kernel(place_ref, *refs):
    sources, rest = refs[:9], refs[9:]
    out_ref, items, wv_t, wo, gain, wm, own, mine, rest = *rest[:8], rest[8:]
    lists, queries, wq, wk, wv, ids, ids_smem, sems = rest
    blocks = out_ref.shape[0]
    count = mine.shape[0]
    lists_ref, queries_ref, wq_ref, wk_ref, wv_ref, wo_ref, gain_ref, wm_ref, own_ref = sources
    mine_ref = queries_ref.at[pl.ds(pl.multiple_of(place_ref[1] * count, count), count)]
    moves = [(lists_ref, lists), (queries_ref, queries), (wq_ref, wq), (wk_ref, wk), (wv_ref, wv)]
    moves += [(wo_ref, wo), (gain_ref, gain), (wm_ref, wm), (own_ref, own), (mine_ref, mine)]
    copies = [pltpu.make_async_copy(source, target, sems.at[i]) for i, (source, target) in enumerate(moves)]
    for copy in copies:
        copy.start()
    copies[0].wait()
    code = local_lists(place_ref, lists[...])
    list_row = lax.broadcasted_iota(jnp.int32, code.shape, 1)
    lane = lax.broadcasted_iota(jnp.int32, (code.shape[0], 128), 1)
    for b in range(blocks):
        wanted = place_ref[0] * blocks + b
        listed = jnp.sum(jnp.where(list_row == wanted, code, 0.0), axis=1, keepdims=True).astype(jnp.int32)
        slot = jnp.where(listed < 0, -1, lax.div(listed, 128))
        found = jnp.where(slot == lane, lax.rem(listed, 128), 0)
        phase = jnp.where(slot < 0, -1, lax.div(slot, WIDTH))
        found = found + jnp.where(phase == lane - COUNTS, jnp.where(phase < 0, 0, 1), 0)
        ids[b : b + 1, :] = jnp.sum(found.astype(F32), axis=0, keepdims=True).astype(jnp.int32)
    tell = pltpu.make_async_copy(ids, ids_smem, sems.at[len(moves)])
    tell.start()
    for copy in copies[1:]:
        copy.wait()
    wv_t[...] = wv[...].T
    proj = jnp.dot(queries[...], wq[...], preferred_element_type=F32).astype(BF16)
    head = head_of_lane((QBLK, D))
    scale = LOG2E / math.sqrt(HD)
    none = jnp.zeros((QBLK, D), BF16)
    for b in range(blocks):
        rows = proj[b * QBLK : (b + 1) * QBLK]
        for c in range(PAIRS):
            two = [jnp.where(head == h, rows, none) for h in (2 * c, 2 * c + 1)]
            folded = lax.dot_general(wk[...], jnp.concatenate(two, axis=0), NT, preferred_element_type=F32)
            out_ref[b, :, c * WIDE : (c + 1) * WIDE] = (folded * scale).astype(BF16)
    tell.wait()
    write_items(ids_smem, items, blocks)


def project(place, count, lists, queries, w_query, w_key, w_value, w_out, norm_gain, w_mask, features):
    blocks = queries.shape[0] // QBLK
    square = jax.ShapeDtypeStruct((D, D), BF16)
    gain = norm_gain.reshape(1, D)
    return pl.pallas_call(
        project_kernel,
        out_shape=(
            jax.ShapeDtypeStruct((blocks, D, H * QBLK), BF16),
            jax.ShapeDtypeStruct((8, 128), jnp.int32),
            square,
            square,
            jax.ShapeDtypeStruct(gain.shape, F32),
            square,
            jax.ShapeDtypeStruct(features.shape, BF16),
            jax.ShapeDtypeStruct((count, D), BF16),
        ),
        in_specs=[IN_SMEM] + [IN_HBM] * 9,
        out_specs=(IN_VMEM, IN_SMEM) + (IN_VMEM,) * 6,
        scratch_shapes=[
            pltpu.VMEM(lists.shape, jnp.int32),
            pltpu.VMEM(queries.shape, BF16),
            pltpu.VMEM((D, D), BF16),
            pltpu.VMEM((D, D), BF16),
            pltpu.VMEM((D, D), BF16),
            pltpu.VMEM((blocks, 128), jnp.int32),
            pltpu.SMEM((blocks, 128), jnp.int32),
            pltpu.SemaphoreType.DMA((11,)),
        ],
        compiler_params=pltpu.CompilerParams(vmem_limit_bytes=16 * MIB),
        cost_estimate=pl.CostEstimate(
            flops=2 * queries.shape[0] * D * D * (H + 1), bytes_accessed=3 * MIB, transcendentals=0
        ),
        name="project",
    )(place, *map(stay, (lists, queries, w_query, w_key, w_value, w_out, gain, w_mask, features)))


def keys_of(item, feats):
    rows = [lax.rem(lax.div(item, 16 * step), 64) * SBLK for step in (1, 64)]
    return jnp.concatenate([feats[pl.ds(pl.multiple_of(row, SBLK), SBLK), :] for row in rows], axis=0)


def score(item, feats, q_ref, scores):
    b = jnp.minimum(lax.rem(item, 16), q_ref.shape[0] - 1)
    scores[...] = jnp.dot(keys_of(item, feats), q_ref[b], preferred_element_type=F32)


def weigh(item, feats, scores, acc, stats):
    b = lax.rem(item, 16)
    turned = keys_of(item, feats).T
    alone = lax.div(item, 16 * 64 * 64) == 1
    halves = H * QBLK // 2
    for c in range(2):
        part = slice(c * halves, (c + 1) * halves)
        first = scores[:SBLK, part]
        second = jnp.where(alone, -jnp.inf, scores[SBLK:, part])
        top = stats[b, 0:1, part]
        higher = jnp.maximum(top, jnp.max(jnp.maximum(first, second), axis=0, keepdims=True))
        factor = jnp.exp2(top - higher)
        first = jnp.exp2(first - higher)
        second = jnp.exp2(second - higher)
        stats[b, 0:1, part] = higher
        stats[b, 1:2, part] = stats[b, 1:2, part] * factor + jnp.sum(first + second, axis=0, keepdims=True)
        weights = jnp.concatenate([first.astype(BF16), second.astype(BF16)], axis=0)
        acc[b, :, part] = acc[b, :, part] * factor + jnp.dot(turned, weights, preferred_element_type=F32)


def attend_kernel(phase, sizes, last, items, q_ref, *rest):
    count = len(sizes)
    piece_refs, rest = rest[:count], rest[count:]
    if phase:
        rest = rest[2:]
    if last:
        wv_t, acc, stats_ref, out_ref, feats, even, odd = rest
    else:
        acc, stats_ref, feats, even, odd = rest
    held = 0
    for size, ref in zip(sizes, piece_refs):
        feats[held : held + size, :] = ref[...]
        held += size
    if phase == 0:
        acc[...] = jnp.zeros(acc.shape, F32)
        stats_ref[:, 0:1, :] = jnp.full((acc.shape[0], 1, H * QBLK), -jnp.inf, F32)
        stats_ref[:, 1:2, :] = jnp.zeros((acc.shape[0], 1, H * QBLK), F32)
    score(items[phase, 0], feats, q_ref, even)

    def two_items(i, carry):
        score(items[phase, 2 * i + 1], feats, q_ref, odd)
        weigh(items[phase, 2 * i], feats, even, acc, stats_ref)
        score(items[phase, 2 * i + 2], feats, q_ref, even)
        weigh(items[phase, 2 * i + 1], feats, odd, acc, stats_ref)
        return carry

    lax.fori_loop(0, lax.div(items[phase, LAST] + 1, 2), two_items, 0)
    if not last:
        return
    slot = lax.broadcasted_iota(jnp.int32, (16, WIDE), 0)
    column = lax.broadcasted_iota(jnp.int32, (QBLK, D + TAIL), 1)
    odd_head = jnp.where(column < D, lax.rem(lax.div(column, HD), 2), lax.rem(lax.div(column, 16), 2))
    empty = jnp.zeros((TAIL - 32, WIDE), F32)
    for b in range(q_ref.shape[0]):
        diagonal = []
        tail = jnp.zeros((16, WIDE), F32)
        for c in range(PAIRS):
            part = slice(c * WIDE, (c + 1) * WIDE)
            total = stats_ref[b, 1:2, part]
            mean = (acc[b, :, part] * (1.0 / total)).astype(BF16)
            heads = slice(2 * HD * c, 2 * HD * (c + 1))
            diagonal.append(jnp.dot(wv_t[heads, :], mean, preferred_element_type=F32))
            level = stats_ref[b, 0:1, part] + jnp.log(total) * LOG2E
            for piece in range(3):
                rounded = level.astype(BF16).astype(F32)
                level = level - rounded
                tail = jnp.where(slot == piece * PAIRS + c, rounded, tail)
        turned = jnp.concatenate(diagonal + [tail, tail, empty], axis=0).T
        rows = jnp.where(odd_head == 1, turned[QBLK:], turned[:QBLK])
        out_ref[b * QBLK : (b + 1) * QBLK, :] = rows.astype(BF16)


def attend(phase, items, folded, arrays, state, wv_t):
    blocks = folded.shape[0]
    last = wv_t is not None
    sizes = [a.shape[0] for a in arrays]
    out_shape = [
        jax.ShapeDtypeStruct((blocks + 1, D, H * QBLK), F32),
        jax.ShapeDtypeStruct((blocks + 1, 8, H * QBLK), F32),
    ]
    args = [items, folded, *arrays]
    in_specs = [IN_SMEM, IN_VMEM] + [IN_VMEM] * len(arrays)
    scratch = [pltpu.VMEM((sum(sizes), D), BF16)] + [pltpu.VMEM((2 * SBLK, H * QBLK), F32)] * 2
    aliases = {}
    if phase:
        aliases = {len(args): 0, len(args) + 1: 1}
        args += list(state)
        in_specs += [IN_VMEM] * 2
    if last:
        args.append(wv_t)
        in_specs.append(IN_VMEM)
        out_shape.append(jax.ShapeDtypeStruct((blocks * QBLK, D + TAIL), BF16))
    return pl.pallas_call(
        functools.partial(attend_kernel, phase, sizes, last),
        out_shape=out_shape,
        in_specs=in_specs,
        out_specs=[IN_VMEM] * len(out_shape),
        input_output_aliases=aliases,
        scratch_shapes=scratch,
        compiler_params=pltpu.CompilerParams(vmem_limit_bytes=16 * MIB),
        cost_estimate=pl.CostEstimate(flops=1_000_000_000, bytes_accessed=4 * MIB, transcendentals=700_000),
        name="attend_%d" % phase,
    )(*args)


def finish_kernel(got_ref, queries, wo, gain, out_ref):
    sources, count, _ = got_ref.shape
    slot = lax.broadcasted_iota(jnp.int32, (TAIL, D), 0)
    pairs = H // 2
    head = 2 * lax.rem(slot, pairs) + lax.div(slot, 16)
    spread = (head == head_of_lane((TAIL, D))) & (lax.rem(slot, 16) < 3 * pairs) & (slot < 32)
    spread = jnp.where(spread, 1.0, 0.0).astype(BF16)
    tails = got_ref[:, :, D:].reshape(sources * count, TAIL)
    levels = jnp.dot(tails, spread, preferred_element_type=F32).reshape(sources, count, D)
    factors = jnp.exp2(levels - jnp.max(levels, axis=0, keepdims=True))
    mixed = jnp.sum(factors * got_ref[:, :, :D].astype(F32), axis=0)
    attended = (mixed / jnp.sum(factors, axis=0)).astype(BF16)
    rows = queries[...].astype(F32) + jnp.dot(attended, wo[...], preferred_element_type=F32)
    center = rows - jnp.mean(rows, axis=1, keepdims=True)
    variance = jnp.mean(center * center, axis=1, keepdims=True)
    updated = (center * lax.rsqrt(variance + 1e-05) * gain[...]).astype(BF16)
    for i in range(sources):
        out_ref[i] = updated


def finish(got, queries, w_out, norm_gain):
    sources, count, _ = got.shape
    return pl.pallas_call(
        finish_kernel,
        out_shape=jax.ShapeDtypeStruct((sources, count, D), BF16),
        in_specs=[IN_VMEM] * 4,
        out_specs=IN_VMEM,
        compiler_params=pltpu.CompilerParams(vmem_limit_bytes=16 * MIB),
        cost_estimate=pl.CostEstimate(flops=10_000_000, bytes_accessed=MIB, transcendentals=140_000),
        name="finish",
    )(got, queries, w_out, norm_gain)


STEP = 512
SLOTS = 4


def piece_row(place_ref, piece):
    ahead, other, row = piece
    index = place_ref[0]
    chip = lax.rem(lax.div(index, 2) + ahead + CHIPS, CHIPS)
    core = lax.rem(index, 2)
    core = 1 - core if other else core
    return (chip * 2 + core) * (OWN_BLOCKS * SBLK) + row


def logits_kernel(pieces, place_ref, updated_ref, wm, *rest):
    count = len(pieces)
    piece_refs = rest[:count]
    updated_out, out_ref, embed, tiles, in_sems, out_sems = rest[count:]
    keep = pltpu.make_async_copy(updated_ref, updated_out, in_sems.at[0])
    keep.start()
    rows = jnp.dot(updated_ref[...], wm[...], preferred_element_type=F32).astype(BF16)
    embed[...] = rows * (1.0 / math.sqrt(D))
    stores = []
    for i, ref in enumerate(piece_refs):
        for row in range(0, ref.shape[0], STEP):
            slot = len(stores) % SLOTS
            if len(stores) >= SLOTS:
                stores[-SLOTS].wait()
            tiles[slot] = lax.dot_general(
                embed[...], ref[row : row + STEP, :], NT, preferred_element_type=F32
            )
            column = pl.multiple_of(piece_row(place_ref, pieces[i]) + row, STEP)
            stores.append(
                pltpu.make_async_copy(tiles.at[slot], out_ref.at[:, pl.ds(column, STEP)], out_sems.at[slot])
            )
            stores[-1].start()
    for store in stores[-SLOTS:]:
        store.wait()
    keep.wait()


def logits(place, updated, w_mask, pieces, arrays):
    count = updated.shape[0]
    shard = sum(a.shape[0] for a in arrays)
    return pl.pallas_call(
        functools.partial(logits_kernel, pieces),
        out_shape=(
            jax.ShapeDtypeStruct(updated.shape, BF16),
            jax.ShapeDtypeStruct((count, shard), F32),
        ),
        in_specs=[IN_SMEM, IN_VMEM, IN_VMEM] + [IN_VMEM] * len(arrays),
        out_specs=(IN_HBM, IN_HBM),
        scratch_shapes=[
            pltpu.VMEM((count, D), BF16),
            pltpu.VMEM((SLOTS, count, STEP), F32),
            pltpu.SemaphoreType.DMA((1,)),
            pltpu.SemaphoreType.DMA((SLOTS,)),
        ],
        compiler_params=pltpu.CompilerParams(vmem_limit_bytes=16 * MIB),
        cost_estimate=pl.CostEstimate(
            flops=2 * count * shard * D, bytes_accessed=20 * MIB, transcendentals=0
        ),
        name="logits",
    )(place, updated, w_mask, *arrays)


def tied(first, second, state):
    first, state = lax.optimization_barrier((first, tuple(state)))
    second, state = lax.optimization_barrier((second, state))
    return first, second, state


def shards(queries, features, block_lists, w_query, w_key, w_value, w_out, norm_gain, w_mask):
    space = lax.axis_size("space")
    place = jnp.stack([lax.axis_index("query"), lax.axis_index("space")]).astype(jnp.int32)
    up = [(y * 2 + c, (y + 1) % CHIPS * 2 + c) for y in range(CHIPS) for c in range(2)]
    down = [(y * 2 + c, (y - 1) % CHIPS * 2 + c) for y in range(CHIPS) for c in range(2)]
    cores = [(i, i ^ 1) for i in range(2 * CHIPS)]

    def send(rows, pairs):
        return lax.ppermute(rows, "query", pairs)

    below = send(features, up)
    above = send(features, down)
    beside = send(features, cores)
    count = queries.shape[0] // space
    weights = (w_query, w_key, w_value, w_out, norm_gain, w_mask)
    folded, items, wv_t, w_out, norm_gain, w_mask, own, mine = project(
        place, count, block_lists.T, queries, *weights, features
    )
    state = attend(0, items, folded, [own, beside], None, None)
    half = features.shape[0] // 2
    below, above, state = tied(below, above, state)
    far_low = send(below[:half], up)
    far_high = send(above[half:], down)
    sent = lax.optimization_barrier((below, above))
    near = [below, send(sent[0], cores), above, send(sent[1], cores)]
    state = attend(1, items, folded, near, state, None)
    far_low, far_high, state = tied(far_low, far_high, state)
    far = [far_low, send(far_low, cores), far_high, send(far_high, cores)]
    partial = attend(2, items, folded, far, state, wv_t)[2]

    got = lax.all_to_all(partial.reshape(space, count, D + TAIL), "space", 0, 0)
    rows = finish(got, mine, w_out, norm_gain)
    updated = lax.all_to_all(rows, "space", 0, 0).reshape(queries.shape)
    pieces = [(0, False, 0), (0, True, 0), (-1, False, 0), (-1, True, 0), (1, False, 0), (1, True, 0)]
    pieces += [(-2, False, 0), (-2, True, 0), (2, False, half), (2, True, half)]
    return logits(place, updated, w_mask, pieces, [own, beside, *near, *far])


def solution(mesh):
    placed = (P("query", None), P(("space", "query"), None), P(), P(), P(), P(), P(), P(), P())
    return jax.shard_map(
        shards,
        mesh=mesh,
        in_specs=placed,
        out_specs=(P("query", None), P("query", "space")),
        check_vma=False,
    )
```

time: 73.7 us -> 69.8 us (0.947); the launches traced: 73.7 us -> 68.9 us
  local copies, waits for them, and re-layouts: 4.6 us -> 0.04 us
  Pallas kernels: 25.5 us -> 22.4 us
  starting transfers between devices: 6.37 us -> 7.79 us
  waiting for transfers between devices: 7.25 us -> 8.25 us
    unnamed x22 -> x0, local copies, waits for them, and re-layouts: 4.56 us -> none
    pallas_call x3, Pallas kernels: 13.3 us -> 9.91 us  [attend(): pl.pallas_call(functools.partial(attend_kernel, phase, sizes, last), out_...]
    ppermute x9, starting transfers between devices: 6.37 us -> 7.79 us  [send(): return lax.ppermute(rows, 'query', pairs)]
    pallas_call x1, Pallas kernels: 3.58 us -> 4.82 us  [project(): pl.pallas_call(project_kernel, out_shape=(jax.ShapeDtypeStruct((blocks, D...]
    ppermute x9, waiting for transfers between devices: 7.25 us -> 8.25 us  [send(): return lax.ppermute(rows, 'query', pairs)]
    pallas_call x1, Pallas kernels: 1.43 us -> 0.63 us  [finish(): pl.pallas_call(finish_kernel, out_shape=jax.ShapeDtypeStruct((sources, co...]
  transfers between devices with their start and end apart: 9 -> 9, of which waited for: 6 -> 5; matrix products, arithmetic and copies ran while one was open for 0% -> 0% of each run, Pallas kernels for 17% -> 17%
where the time goes in v2:
time: 69.8 us; the launch traced here: 68.9 us
  blocking collectives  29.6 us (42%)
  Pallas kernels  22.4 us (32%)
  waiting for transfers between devices  8.25 us (12%)
  starting transfers between devices  7.79 us (11%)
  between operations  0.7 us (1%)
    all_to_all x1, blocking collectives, shards(): got = lax.all_to_all(partial.reshape(space, count, D + TAIL), 'space', 0, 0)  17.6 us
    all_to_all x1, blocking collectives, shards(): updated = lax.all_to_all(rows, 'space', 0, 0).reshape(queries.shape)  12 us
    pallas_call x3, Pallas kernels, attend(): pl.pallas_call(functools.partial(attend_kernel, phase, sizes, last), out_...  9.91 us
    ppermute x9, waiting for transfers between devices, send(): return lax.ppermute(rows, 'query', pairs)  8.25 us
    ppermute x9, starting transfers between devices, send(): return lax.ppermute(rows, 'query', pairs)  7.79 us
    pallas_call x1, Pallas kernels, logits(): pl.pallas_call(functools.partial(logits_kernel, pieces), out_shape=(jax.S...  7.05 us
    pallas_call x1, Pallas kernels, project(): pl.pallas_call(project_kernel, out_shape=(jax.ShapeDtypeStruct((blocks, D...  4.82 us
  transfers between devices with their start and end apart: 9, of which 5 were waited for; matrix products, arithmetic and copies ran while one was open for 0% of the time, Pallas kernels for 17%

profile of v2, /device:TPU:0, one launch (start us, length us, event | category | flops | bytes accessed | tf_op | source)
XLA Modules:
  0.0 68.9 jit_solution(5833129043029297022)
XLA Ops:
  0.6 0.1 collective-permute-start.1
  0.7 1.7 %collective-permute-start = (bf16[1024,256]{1,0:T(8,128)(2,1)}, bf16[1024,256]{1,0:T(8,128)(2,1)S(1)}, u32[]{:S(2)}, u32[]{:S(2)}) collective-permute-start(bf16[1024,256]{1,0:T(8,128)(2,1)} %refs_8_.1), channel_id=1, source_target_pairs={{0,32},{16,48},{32,64},{48,80},{64,96},{80,112},{96,0},{112,16},{1... | collective-permute-start | bytes 1572872 | tf_op jit(solution)/shard_map/ppermute | solution.py:398
  2.5 1.6 %collective-permute-start.3 = (bf16[1024,256]{1,0:T(8,128)(2,1)}, bf16[1024,256]{1,0:T(8,128)(2,1)S(1)}, u32[]{:S(2)}, u32[]{:S(2)}) collective-permute-start(bf16[1024,256]{1,0:T(8,128)(2,1)} %refs_8_.1), channel_id=1, source_target_pairs={{0,96},{16,112},{32,0},{48,16},{64,32},{80,48},{96,64},{112,80},{1... | collective-permute-start | bytes 1572872 | tf_op jit(solution)/shard_map/ppermute | solution.py:398
  4.0 0.1 pad_add_fusion.place_ref
  4.1 4.8 %project.1 = (bf16[8,256,512]{2,1,0:T(8,128)(2,1)S(1)}, s32[8,128]{1,0:T(8,128)S(1)}, bf16[256,256]{1,0:T(8,128)(2,1)S(1)}, bf16[256,256]{1,0:T(8,128)(2,1)S(1)}...) custom-call(s32[2]{0:T(128)S(1)} %pad_add_fusion.place_ref, ...), custom_call_target="tpu_custom_call" | custom-call | flops 603979776 | bytes 3145728 | tf_op jit(solution)/shard_map/project/pallas_call | solution.py:139
  8.9 0.0 collective-permute-done.1.rest_1_
  8.9 2.4 %attend_0.1 = (f32[9,256,512]{2,1,0:T(8,128)S(1)}, f32[9,8,512]{2,1,0:T(8,128)S(1)}) custom-call(s32[8,128]{1,0:T(8,128)S(1)} %get-tuple-element.29.items, bf16[8,256,512]{2,1,0:T(8,128)(2,1)S(1)} %get-tuple-element.30.q_ref, bf16[1024,256]{1,0:T(8,128)(2,1)S(1)} %get-tuple-element.31.rest_0_, bf16[1024,256]{1,0:T(8,128)(2,1)S(1)} %collective-permute-done.1.rest_1_), custom_call_target="tpu_custom_call" | custom-call | flops 1000000000 | bytes 4194304 | tf_op jit(solution)/shard_map/attend_0/pallas_call | solution.py:273
  11.4 5.2 %collective-permute-done.rest_0_.rest_2_ = bf16[1024,256]{1,0:T(8,128)(2,1)S(1)} collective-permute-done((bf16[1024,256]{1,0:T(8,128)(2,1)}, bf16[1024,256]{1,0:T(8,128)(2,1)S(1)}, u32[]{:S(2)}, u32[]{:S(2)}) %collective-permute-start) | collective-permute-done | bytes 524320 | tf_op jit(solution)/shard_map/ppermute | solution.py:398
  16.6 0.0 collective-permute-done.3.rest_2_.rest_4_
  16.7 0.0 collective-permute-start.4
  16.7 0.5 collective-permute-start.5
  17.2 1.6 %collective-permute-start.2 = (bf16[512,256]{1,0:T(8,128)(2,1)S(1)}, bf16[512,256]{1,0:T(8,128)(2,1)S(1)}, u32[]{:S(2)}, u32[]{:S(2)}) collective-permute-start(bf16[512,256]{1,0:T(8,128)(2,1)S(1)} %slice.6), channel_id=1, source_target_pairs={{0,32},{16,48},{32,64},{48,80},{64,96},{80,112},{96,0},{112,16},{1... | collective-permute-start | bytes 786440 | tf_op jit(solution)/shard_map/ppermute | solution.py:398
  18.9 1.7 %collective-permute-start.7 = (bf16[512,256]{1,0:T(8,128)(2,1)S(1)}, bf16[512,256]{1,0:T(8,128)(2,1)S(1)}, u32[]{:S(2)}, u32[]{:S(2)}) collective-permute-start(bf16[512,256]{1,0:T(8,128)(2,1)S(1)} %slice.7), channel_id=1, source_target_pairs={{0,96},{16,112},{32,0},{48,16},{64,32},{80,48},{96,64},{112,80},{1... | collective-permute-start | bytes 786440 | tf_op jit(solution)/shard_map/ppermute | solution.py:398
  20.6 0.0 collective-permute-done.4.rest_1_.rest_3_
  20.6 0.0 collective-permute-done.5.rest_3_.rest_5_
  20.6 4.7 %attend_1.1 = (f32[9,256,512]{2,1,0:T(8,128)S(1)}, f32[9,8,512]{2,1,0:T(8,128)S(1)}) custom-call(s32[8,128]{1,0:T(8,128)S(1)} %get-tuple-element.29.items, bf16[8,256,512]{2,1,0:T(8,128)(2,1)S(1)} %get-tuple-element.30.q_ref, bf16[1024,256]{1,0:T(8,128)(2,1)S(1)} %collective-permute-done.rest_0_.rest_2_, ...), custom_call_target="tpu_custom_call", output_to_operand_aliasing={{0}: (6, {}), {1}: (7, {})} | custom-call | flops 1000000000 | bytes 4194304 | tf_op jit(solution)/shard_map/attend_1/pallas_call | solution.py:273
  25.3 1.4 %collective-permute-done.2.rest_0_.rest_6_ = bf16[512,256]{1,0:T(8,128)(2,1)S(1)} collective-permute-done((bf16[512,256]{1,0:T(8,128)(2,1)S(1)}, bf16[512,256]{1,0:T(8,128)(2,1)S(1)}, u32[]{:S(2)}, u32[]{:S(2)}) %collective-permute-start.2) | collective-permute-done | bytes 262176 | tf_op jit(solution)/shard_map/ppermute | solution.py:398
  26.7 0.2 collective-permute-done.7.rest_2_.rest_8_
  26.9 0.0 collective-permute-start.8
  26.9 0.5 collective-permute-start.6
  27.4 1.0 %collective-permute-done.8.rest_3_.rest_9_ = bf16[512,256]{1,0:T(8,128)(2,1)S(1)} collective-permute-done((bf16[512,256]{1,0:T(8,128)(2,1)S(1)}, bf16[512,256]{1,0:T(8,128)(2,1)S(1)}, u32[]{:S(2)}, u32[]{:S(2)}) %collective-permute-start.8) | collective-permute-done | bytes 262176 | tf_op jit(solution)/shard_map/ppermute | solution.py:398
  28.4 0.4 collective-permute-done.6.rest_1_.rest_7_
  28.8 2.8 %attend_2.1 = (f32[9,256,512]{2,1,0:T(8,128)S(1)}, f32[9,8,512]{2,1,0:T(8,128)S(1)}, bf16[512,384]{1,0:T(8,128)(2,1)S(1)}) custom-call(s32[8,128]{1,0:T(8,128)S(1)} %get-tuple-element.29.items, bf16[8,256,512]{2,1,0:T(8,128)(2,1)S(1)} %get-tuple-element.30.q_ref, ...), custom_call_target="tpu_custom_call", output_to_operand_aliasing={{0}: (6, {}), {1}: (7, {})} | custom-call | flops 1000000000 | bytes 4194304 | tf_op jit(solution)/shard_map/attend_2/pallas_call | solution.py:273
  31.6 17.6 %all_to_all.10.got_ref = bf16[16,32,384]{2,1,0:T(8,128)(2,1)S(1)} all-to-all(bf16[16,32,384]{2,1,0:T(8,128)(2,1)S(1)} %bitcast.6), channel_id=1, replica_groups=mesh['query'=8,'space'=16] {'space'}, dimensions={0} | all-to-all | bytes 786432 | tf_op jit(solution)/shard_map/all_to_all | solution.py:420
  49.2 0.6 finish.1
  49.8 12.0 %all_to_all.11 = bf16[16,32,256]{2,1,0:T(8,128)(2,1)S(1)} all-to-all(bf16[16,32,256]{2,1,0:T(8,128)(2,1)S(1)} %finish.1), channel_id=1, replica_groups=mesh['query'=8,'space'=16] {'space'}, dimensions={0} | all-to-all | bytes 524288 | tf_op jit(solution)/shard_map/all_to_all | solution.py:422
  61.8 7.1 %logits.1 = (bf16[512,256]{1,0:T(8,128)(2,1)}, f32[512,8192]{1,0:T(8,128)}) custom-call(s32[2]{0:T(128)S(1)} %pad_add_fusion.place_ref, bf16[512,256]{1,0:T(8,128)(2,1)S(1)} %bitcast.7, bf16[256,256]{1,0:T(8,128)(2,1)S(1)} %get-tuple-element.55.wm, bf16[1024,256]{1,0:T(8,128)(2,1)S(1)} %get-tuple-element.31.rest_0_, ...), custom_call_target="tpu_custom_call" | custom-call | flops 2147483648 | bytes 20971520 | tf_op jit(solution)/shard_map/logits/pallas_call | solution.py:362
  (2 shorter events, 0.0 us)
Async XLA Ops:
  0.6 8.3 %collective-permute-start.1 = (bf16[1024,256]{1,0:T(8,128)(2,1)}, bf16[1024,256]{1,0:T(8,128)(2,1)S(1)}, u32[]{:S(2)}, u32[]{:S(2)}) collective-permute-start(bf16[1024,256]{1,0:T(8,128)(2,1)} %refs_8_.1), channel_id=1, source_target_pairs={{0,16},{16,0},{32,48},{48,32},{64,80},{80,64},{96,112},{112,96},{1... | collective-permute-start | bytes 1572872 | tf_op jit(solution)/shard_map/ppermute | solution.py:398
  0.7 15.9 %collective-permute-start = (bf16[1024,256]{1,0:T(8,128)(2,1)}, bf16[1024,256]{1,0:T(8,128)(2,1)S(1)}, u32[]{:S(2)}, u32[]{:S(2)}) collective-permute-start(bf16[1024,256]{1,0:T(8,128)(2,1)} %refs_8_.1), channel_id=1, source_target_pairs={{0,32},{16,48},{32,64},{48,80},{64,96},{80,112},{96,0},{112,16},{1... | collective-permute-start | bytes 1572872 | tf_op jit(solution)/shard_map/ppermute | solution.py:398
  2.5 14.2 %collective-permute-start.3 = (bf16[1024,256]{1,0:T(8,128)(2,1)}, bf16[1024,256]{1,0:T(8,128)(2,1)S(1)}, u32[]{:S(2)}, u32[]{:S(2)}) collective-permute-start(bf16[1024,256]{1,0:T(8,128)(2,1)} %refs_8_.1), channel_id=1, source_target_pairs={{0,96},{16,112},{32,0},{48,16},{64,32},{80,48},{96,64},{112,80},{1... | collective-permute-start | bytes 1572872 | tf_op jit(solution)/shard_map/ppermute | solution.py:398
  16.7 3.9 %collective-permute-start.4 = (bf16[1024,256]{1,0:T(8,128)(2,1)S(1)}, bf16[1024,256]{1,0:T(8,128)(2,1)S(1)}, u32[]{:S(2)}, u32[]{:S(2)}) collective-permute-start(bf16[1024,256]{1,0:T(8,128)(2,1)S(1)} %collective-permute-done.rest_0_.rest_2_), channel_id=1, source_target_pairs={{0,16},{16,0},{32,48},{48,32},{64,80},{80,64},{96,112},{112,96},{1... | collective-permute-start | bytes 1572872 | tf_op jit(solution)/shard_map/ppermute | solution.py:398
  16.7 3.9 %collective-permute-start.5 = (bf16[1024,256]{1,0:T(8,128)(2,1)S(1)}, bf16[1024,256]{1,0:T(8,128)(2,1)S(1)}, u32[]{:S(2)}, u32[]{:S(2)}) collective-permute-start(bf16[1024,256]{1,0:T(8,128)(2,1)S(1)} %collective-permute-done.3.rest_2_.rest_4_), channel_id=1, source_target_pairs={{0,16},{16,0},{32,48},{48,32},{64,80},{80,64},{96,112},{112,96},{1... | collective-permute-start | bytes 1572872 | tf_op jit(solution)/shard_map/ppermute | solution.py:398
  17.2 9.5 %collective-permute-start.2 = (bf16[512,256]{1,0:T(8,128)(2,1)S(1)}, bf16[512,256]{1,0:T(8,128)(2,1)S(1)}, u32[]{:S(2)}, u32[]{:S(2)}) collective-permute-start(bf16[512,256]{1,0:T(8,128)(2,1)S(1)} %slice.6), channel_id=1, source_target_pairs={{0,32},{16,48},{32,64},{48,80},{64,96},{80,112},{96,0},{112,16},{1... | collective-permute-start | bytes 786440 | tf_op jit(solution)/shard_map/ppermute | solution.py:398
  18.9 8.0 %collective-permute-start.7 = (bf16[512,256]{1,0:T(8,128)(2,1)S(1)}, bf16[512,256]{1,0:T(8,128)(2,1)S(1)}, u32[]{:S(2)}, u32[]{:S(2)}) collective-permute-start(bf16[512,256]{1,0:T(8,128)(2,1)S(1)} %slice.7), channel_id=1, source_target_pairs={{0,96},{16,112},{32,0},{48,16},{64,32},{80,48},{96,64},{112,80},{1... | collective-permute-start | bytes 786440 | tf_op jit(solution)/shard_map/ppermute | solution.py:398
  26.9 1.5 %collective-permute-start.8 = (bf16[512,256]{1,0:T(8,128)(2,1)S(1)}, bf16[512,256]{1,0:T(8,128)(2,1)S(1)}, u32[]{:S(2)}, u32[]{:S(2)}) collective-permute-start(bf16[512,256]{1,0:T(8,128)(2,1)S(1)} %collective-permute-done.7.rest_2_.rest_8_), channel_id=1, source_target_pairs={{0,16},{16,0},{32,48},{48,32},{64,80},{80,64},{96,112},{112,96},{1... | collective-permute-start | bytes 786440 | tf_op jit(solution)/shard_map/ppermute | solution.py:398
  26.9 1.9 %collective-permute-start.6 = (bf16[512,256]{1,0:T(8,128)(2,1)S(1)}, bf16[512,256]{1,0:T(8,128)(2,1)S(1)}, u32[]{:S(2)}, u32[]{:S(2)}) collective-permute-start(bf16[512,256]{1,0:T(8,128)(2,1)S(1)} %collective-permute-done.2.rest_0_.rest_6_), channel_id=1, source_target_pairs={{0,16},{16,0},{32,48},{48,32},{64,80},{80,64},{96,112},{112,96},{1... | collective-permute-start | bytes 786440 | tf_op jit(solution)/shard_map/ppermute | solution.py:398

commit v3 on v2

--- a/solution.py
+++ b/solution.py
@@ -49,11 +49,11 @@
     device = lax.rem(lax.div(lists, OWN_BLOCKS), 2 * CHIPS)
     other = jnp.where(lax.rem(device, 2) == core, 0, 1)
     ahead = lax.rem(lax.div(device, 2) - chip + CHIPS, CHIPS)
-    near = jnp.where(ahead == 1, 2, 0) * OWN_BLOCKS + other * OWN_BLOCKS + inside
-    half = OWN_BLOCKS // 2
-    far = lax.div(inside, half) * OWN_BLOCKS + other * half + lax.rem(inside, half)
-    position = jnp.where(ahead == 2, far, near)
-    phase = jnp.where(ahead == 0, 0, jnp.where(ahead == 2, 2, 1))
+    toward = jnp.where(core == 0, CHIPS - 1, 1)
+    near = (ahead == 1) | (ahead == CHIPS - 1)
+    late = near & (ahead == toward) & (other == 1)
+    position = jnp.where(near & (ahead != toward), 1 + other, jnp.where(near, 2 * other, other)) * OWN_BLOCKS + inside
+    phase = jnp.where(ahead == 0, 0, jnp.where(near & ~late, 1, 2))
     phase = jnp.where(lax.div(lists, SHARD_BLOCKS) == place_ref[1], phase, -1)
     width = lists.shape[0]
     row = lax.broadcasted_iota(jnp.int32, (width, width), 0)
@@ -321,12 +321,11 @@
 
 
 def piece_row(place_ref, piece):
-    ahead, other, row = piece
-    index = place_ref[0]
-    chip = lax.rem(lax.div(index, 2) + ahead + CHIPS, CHIPS)
-    core = lax.rem(index, 2)
+    ahead, other = piece
+    chip, core = lax.div(place_ref[0], 2), lax.rem(place_ref[0], 2)
+    chip = lax.rem(chip + jnp.where(core == 0, -ahead, ahead) + CHIPS, CHIPS)
     core = 1 - core if other else core
-    return (chip * 2 + core) * (OWN_BLOCKS * SBLK) + row
+    return (chip * 2 + core) * (OWN_BLOCKS * SBLK)
 
 
 def logits_kernel(pieces, place_ref, updated_ref, wm, *rest):
@@ -381,47 +380,38 @@
     )(place, updated, w_mask, *arrays)
 
 
-def tied(first, second, state):
-    first, state = lax.optimization_barrier((first, tuple(state)))
-    second, state = lax.optimization_barrier((second, state))
-    return first, second, state
-
-
 def shards(queries, features, block_lists, w_query, w_key, w_value, w_out, norm_gain, w_mask):
     space = lax.axis_size("space")
     place = jnp.stack([lax.axis_index("query"), lax.axis_index("space")]).astype(jnp.int32)
-    up = [(y * 2 + c, (y + 1) % CHIPS * 2 + c) for y in range(CHIPS) for c in range(2)]
-    down = [(y * 2 + c, (y - 1) % CHIPS * 2 + c) for y in range(CHIPS) for c in range(2)]
+    ring = [(y * 2 + c, (y + 1 - 2 * c) % CHIPS * 2 + c) for y in range(CHIPS) for c in range(2)]
+    back = [(to, source) for source, to in ring]
     cores = [(i, i ^ 1) for i in range(2 * CHIPS)]
 
     def send(rows, pairs):
         return lax.ppermute(rows, "query", pairs)
 
-    below = send(features, up)
-    above = send(features, down)
+    came = send(features, ring)
     beside = send(features, cores)
+    later, beside = lax.optimization_barrier((features, beside))
+    back_came = send(later, back)
     count = queries.shape[0] // space
     weights = (w_query, w_key, w_value, w_out, norm_gain, w_mask)
     folded, items, wv_t, w_out, norm_gain, w_mask, own, mine = project(
         place, count, block_lists.T, queries, *weights, features
     )
     state = attend(0, items, folded, [own, beside], None, None)
-    half = features.shape[0] // 2
-    below, above, state = tied(below, above, state)
-    far_low = send(below[:half], up)
-    far_high = send(above[half:], down)
-    sent = lax.optimization_barrier((below, above))
-    near = [below, send(sent[0], cores), above, send(sent[1], cores)]
+    came, state = lax.optimization_barrier((came, tuple(state)))
+    far = send(came, ring)
+    near = [came, back_came, send(came, cores)]
     state = attend(1, items, folded, near, state, None)
-    far_low, far_high, state = tied(far_low, far_high, state)
-    far = [far_low, send(far_low, cores), far_high, send(far_high, cores)]
+    far, state = lax.optimization_barrier((far, tuple(state)))
+    far = [far, send(far, cores), send(back_came, cores)]
     partial = attend(2, items, folded, far, state, wv_t)[2]
 
     got = lax.all_to_all(partial.reshape(space, count, D + TAIL), "space", 0, 0)
     rows = finish(got, mine, w_out, norm_gain)
     updated = lax.all_to_all(rows, "space", 0, 0).reshape(queries.shape)
-    pieces = [(0, False, 0), (0, True, 0), (-1, False, 0), (-1, True, 0), (1, False, 0), (1, True, 0)]
-    pieces += [(-2, False, 0), (-2, True, 0), (2, False, half), (2, True, half)]
+    pieces = [(0, False), (0, True), (1, False), (-1, False), (-1, True), (2, False), (2, True), (1, True)]
     return logits(place, updated, w_mask, pieces, [own, beside, *near, *far])
 
 

time: 69.8 us -> 68.9 us (0.987)
  Pallas kernels: 22.4 us -> 25 us
  starting transfers between devices: 7.79 us -> 5.83 us
    pallas_call x3, Pallas kernels: 9.91 us -> 12.4 us  [attend(): pl.pallas_call(functools.partial(attend_kernel, phase, sizes, last), out_...]
    ppermute x9 -> x7, starting transfers between devices: 7.79 us -> 5.83 us  [send(): return lax.ppermute(rows, 'query', pairs)]
    ppermute x9 -> x7, waiting for transfers between devices: 8.25 us -> 7.75 us  [send(): return lax.ppermute(rows, 'query', pairs)]
  transfers between devices with their start and end apart: 9 -> 7, of which waited for: 5 -> 4; matrix products, arithmetic and copies ran while one was open for 0% -> 0% of each run, Pallas kernels for 17% -> 18%
where the time goes in v3:
time: 68.9 us; the launch traced here: 68.4 us
  blocking collectives  29.1 us (42%)
  Pallas kernels  25 us (36%)
  waiting for transfers between devices  7.75 us (11%)
  starting transfers between devices  5.83 us (8%)
  between operations  0.7 us (1%)
    all_to_all x1, blocking collectives, shards(): got = lax.all_to_all(partial.reshape(space, count, D + TAIL), 'space', 0, 0)  17.1 us
    pallas_call x3, Pallas kernels, attend(): pl.pallas_call(functools.partial(attend_kernel, phase, sizes, last), out_...  12.4 us
    all_to_all x1, blocking collectives, shards(): updated = lax.all_to_all(rows, 'space', 0, 0).reshape(queries.shape)  12 us
    ppermute x7, waiting for transfers between devices, send(): return lax.ppermute(rows, 'query', pairs)  7.75 us
    pallas_call x1, Pallas kernels, logits(): pl.pallas_call(functools.partial(logits_kernel, pieces), out_shape=(jax.S...  7.05 us
    ppermute x7, starting transfers between devices, send(): return lax.ppermute(rows, 'query', pairs)  5.83 us
    pallas_call x1, Pallas kernels, project(): pl.pallas_call(project_kernel, out_shape=(jax.ShapeDtypeStruct((blocks, D...  4.9 us
  transfers between devices with their start and end apart: 7, of which 4 were waited for; matrix products, arithmetic and copies ran while one was open for 0% of the time, Pallas kernels for 18%

profile of v3, /device:TPU:0, one launch (start us, length us, event | category | flops | bytes accessed | tf_op | source)
XLA Modules:
  0.0 68.4 jit_solution(633073546575531119)
XLA Ops:
  0.6 0.1 collective-permute-start.1
  0.7 1.7 %collective-permute-start = (bf16[1024,256]{1,0:T(8,128)(2,1)}, bf16[1024,256]{1,0:T(8,128)(2,1)S(1)}, u32[]{:S(2)}, u32[]{:S(2)}) collective-permute-start(bf16[1024,256]{1,0:T(8,128)(2,1)} %refs_8_.1), channel_id=1, source_target_pairs={{0,32},{16,112},{32,64},{48,16},{64,96},{80,48},{96,0},{112,80},{1... | collective-permute-start | bytes 1572872 | tf_op jit(solution)/shard_map/ppermute | solution.py:391
  2.5 0.1 pad_add_fusion.place_ref
  2.5 4.9 %project.1 = (bf16[8,256,512]{2,1,0:T(8,128)(2,1)S(1)}, s32[8,128]{1,0:T(8,128)S(1)}, bf16[256,256]{1,0:T(8,128)(2,1)S(1)}, bf16[256,256]{1,0:T(8,128)(2,1)S(1)}...) custom-call(s32[2]{0:T(128)S(1)} %pad_add_fusion.place_ref, ...), custom_call_target="tpu_custom_call" | custom-call | flops 603979776 | bytes 3145728 | tf_op jit(solution)/shard_map/project/pallas_call | solution.py:139
  7.4 0.0 collective-permute-done.1.rest_1_
  7.4 1.5 %collective-permute-start.3 = (bf16[1024,256]{1,0:T(8,128)(2,1)}, bf16[1024,256]{1,0:T(8,128)(2,1)S(1)}, u32[]{:S(2)}, u32[]{:S(2)}) collective-permute-start(bf16[1024,256]{1,0:T(8,128)(2,1)} %refs_8_.1), channel_id=1, source_target_pairs={{32,0},{112,16},{64,32},{16,48},{96,64},{48,80},{0,96},{80,112},{3... | collective-permute-start | bytes 1572872 | tf_op jit(solution)/shard_map/ppermute | solution.py:391
  8.9 3.0 %attend_0.1 = (f32[9,256,512]{2,1,0:T(8,128)S(1)}, f32[9,8,512]{2,1,0:T(8,128)S(1)}) custom-call(s32[8,128]{1,0:T(8,128)S(1)} %get-tuple-element.23.items, bf16[8,256,512]{2,1,0:T(8,128)(2,1)S(1)} %get-tuple-element.24.q_ref, bf16[1024,256]{1,0:T(8,128)(2,1)S(1)} %get-tuple-element.25.rest_0_, bf16[1024,256]{1,0:T(8,128)(2,1)S(1)} %collective-permute-done.1.rest_1_), custom_call_target="tpu_custom_call" | custom-call | flops 1000000000 | bytes 4194304 | tf_op jit(solution)/shard_map/attend_0/pallas_call | solution.py:273
  11.9 0.0 collective-permute-done.rest_0_.rest_2_
  12.0 0.2 collective-permute-start.4
  12.2 1.8 %collective-permute-start.2 = (bf16[1024,256]{1,0:T(8,128)(2,1)S(1)}, bf16[1024,256]{1,0:T(8,128)(2,1)S(1)}, u32[]{:S(2)}, u32[]{:S(2)}) collective-permute-start(bf16[1024,256]{1,0:T(8,128)(2,1)S(1)} %collective-permute-done.rest_0_.rest_2_), channel_id=1, source_target_pairs={{0,32},{16,112},{32,64},{48,16},{64,96},{80,48},{96,0},{112,80},{1... | collective-permute-start | bytes 1572872 | tf_op jit(solution)/shard_map/ppermute | solution.py:391
  14.0 4.5 %collective-permute-done.3.rest_1_.rest_3_ = bf16[1024,256]{1,0:T(8,128)(2,1)S(1)} collective-permute-done((bf16[1024,256]{1,0:T(8,128)(2,1)}, bf16[1024,256]{1,0:T(8,128)(2,1)S(1)}, u32[]{:S(2)}, u32[]{:S(2)}) %collective-permute-start.3) | collective-permute-done | bytes 524320 | tf_op jit(solution)/shard_map/ppermute | solution.py:391
  18.5 0.0 collective-permute-done.4.rest_2_.rest_4_
  18.5 4.7 %attend_1.1 = (f32[9,256,512]{2,1,0:T(8,128)S(1)}, f32[9,8,512]{2,1,0:T(8,128)S(1)}) custom-call(s32[8,128]{1,0:T(8,128)S(1)} %get-tuple-element.23.items, bf16[8,256,512]{2,1,0:T(8,128)(2,1)S(1)} %get-tuple-element.24.q_ref, bf16[1024,256]{1,0:T(8,128)(2,1)S(1)} %collective-permute-done.rest_0_.rest_2_, ...), custom_call_target="tpu_custom_call", output_to_operand_aliasing={{0}: (5, {}), {1}: (6, {})} | custom-call | flops 1000000000 | bytes 4194304 | tf_op jit(solution)/shard_map/attend_1/pallas_call | solution.py:273
  23.2 1.1 %collective-permute-done.2.rest_0_.rest_5_ = bf16[1024,256]{1,0:T(8,128)(2,1)S(1)} collective-permute-done((bf16[1024,256]{1,0:T(8,128)(2,1)S(1)}, bf16[1024,256]{1,0:T(8,128)(2,1)S(1)}, u32[]{:S(2)}, u32[]{:S(2)}) %collective-permute-start.2) | collective-permute-done | bytes 524320 | tf_op jit(solution)/shard_map/ppermute | solution.py:391
  24.3 0.3 collective-permute-start.6
  24.6 0.2 collective-permute-start.5
  24.8 1.4 %collective-permute-done.6.rest_2_.rest_7_ = bf16[1024,256]{1,0:T(8,128)(2,1)S(1)} collective-permute-done((bf16[1024,256]{1,0:T(8,128)(2,1)S(1)}, bf16[1024,256]{1,0:T(8,128)(2,1)S(1)}, u32[]{:S(2)}, u32[]{:S(2)}) %collective-permute-start.6) | collective-permute-done | bytes 524320 | tf_op jit(solution)/shard_map/ppermute | solution.py:391
  26.2 0.7 %collective-permute-done.5.rest_1_.rest_6_ = bf16[1024,256]{1,0:T(8,128)(2,1)S(1)} collective-permute-done((bf16[1024,256]{1,0:T(8,128)(2,1)S(1)}, bf16[1024,256]{1,0:T(8,128)(2,1)S(1)}, u32[]{:S(2)}, u32[]{:S(2)}) %collective-permute-start.5) | collective-permute-done | bytes 524320 | tf_op jit(solution)/shard_map/ppermute | solution.py:391
  26.9 4.7 %attend_2.1 = (f32[9,256,512]{2,1,0:T(8,128)S(1)}, f32[9,8,512]{2,1,0:T(8,128)S(1)}, bf16[512,384]{1,0:T(8,128)(2,1)S(1)}) custom-call(s32[8,128]{1,0:T(8,128)S(1)} %get-tuple-element.23.items, bf16[8,256,512]{2,1,0:T(8,128)(2,1)S(1)} %get-tuple-element.24.q_ref, ...), custom_call_target="tpu_custom_call", output_to_operand_aliasing={{0}: (5, {}), {1}: (6, {})} | custom-call | flops 1000000000 | bytes 4194304 | tf_op jit(solution)/shard_map/attend_2/pallas_call | solution.py:273
  31.6 17.1 %all_to_all.10.got_ref = bf16[16,32,384]{2,1,0:T(8,128)(2,1)S(1)} all-to-all(bf16[16,32,384]{2,1,0:T(8,128)(2,1)S(1)} %bitcast.6), channel_id=1, replica_groups=mesh['query'=8,'space'=16] {'space'}, dimensions={0} | all-to-all | bytes 786432 | tf_op jit(solution)/shard_map/all_to_all | solution.py:411
  48.7 0.6 finish.1
  49.4 12.0 %all_to_all.11 = bf16[16,32,256]{2,1,0:T(8,128)(2,1)S(1)} all-to-all(bf16[16,32,256]{2,1,0:T(8,128)(2,1)S(1)} %finish.1), channel_id=1, replica_groups=mesh['query'=8,'space'=16] {'space'}, dimensions={0} | all-to-all | bytes 524288 | tf_op jit(solution)/shard_map/all_to_all | solution.py:413
  61.4 7.1 %logits.1 = (bf16[512,256]{1,0:T(8,128)(2,1)}, f32[512,8192]{1,0:T(8,128)}) custom-call(s32[2]{0:T(128)S(1)} %pad_add_fusion.place_ref, bf16[512,256]{1,0:T(8,128)(2,1)S(1)} %bitcast.7, bf16[256,256]{1,0:T(8,128)(2,1)S(1)} %get-tuple-element.43.wm, bf16[1024,256]{1,0:T(8,128)(2,1)S(1)} %get-tuple-element.25.rest_0_, ...), custom_call_target="tpu_custom_call" | custom-call | flops 2147483648 | bytes 20971520 | tf_op jit(solution)/shard_map/logits/pallas_call | solution.py:361
Async XLA Ops:
  0.6 6.8 %collective-permute-start.1 = (bf16[1024,256]{1,0:T(8,128)(2,1)}, bf16[1024,256]{1,0:T(8,128)(2,1)S(1)}, u32[]{:S(2)}, u32[]{:S(2)}) collective-permute-start(bf16[1024,256]{1,0:T(8,128)(2,1)} %refs_8_.1), channel_id=1, source_target_pairs={{0,16},{16,0},{32,48},{48,32},{64,80},{80,64},{96,112},{112,96},{1... | collective-permute-start | bytes 1572872 | tf_op jit(solution)/shard_map/ppermute | solution.py:391
  0.7 11.2 %collective-permute-start = (bf16[1024,256]{1,0:T(8,128)(2,1)}, bf16[1024,256]{1,0:T(8,128)(2,1)S(1)}, u32[]{:S(2)}, u32[]{:S(2)}) collective-permute-start(bf16[1024,256]{1,0:T(8,128)(2,1)} %refs_8_.1), channel_id=1, source_target_pairs={{0,32},{16,112},{32,64},{48,16},{64,96},{80,48},{96,0},{112,80},{1... | collective-permute-start | bytes 1572872 | tf_op jit(solution)/shard_map/ppermute | solution.py:391
  7.4 11.0 %collective-permute-start.3 = (bf16[1024,256]{1,0:T(8,128)(2,1)}, bf16[1024,256]{1,0:T(8,128)(2,1)S(1)}, u32[]{:S(2)}, u32[]{:S(2)}) collective-permute-start(bf16[1024,256]{1,0:T(8,128)(2,1)} %refs_8_.1), channel_id=1, source_target_pairs={{32,0},{112,16},{64,32},{16,48},{96,64},{48,80},{0,96},{80,112},{3... | collective-permute-start | bytes 1572872 | tf_op jit(solution)/shard_map/ppermute | solution.py:391
  12.0 6.5 %collective-permute-start.4 = (bf16[1024,256]{1,0:T(8,128)(2,1)S(1)}, bf16[1024,256]{1,0:T(8,128)(2,1)S(1)}, u32[]{:S(2)}, u32[]{:S(2)}) collective-permute-start(bf16[1024,256]{1,0:T(8,128)(2,1)S(1)} %collective-permute-done.rest_0_.rest_2_), channel_id=1, source_target_pairs={{0,16},{16,0},{32,48},{48,32},{64,80},{80,64},{96,112},{112,96},{1... | collective-permute-start | bytes 1572872 | tf_op jit(solution)/shard_map/ppermute | solution.py:391
  12.2 12.1 %collective-permute-start.2 = (bf16[1024,256]{1,0:T(8,128)(2,1)S(1)}, bf16[1024,256]{1,0:T(8,128)(2,1)S(1)}, u32[]{:S(2)}, u32[]{:S(2)}) collective-permute-start(bf16[1024,256]{1,0:T(8,128)(2,1)S(1)} %collective-permute-done.rest_0_.rest_2_), channel_id=1, source_target_pairs={{0,32},{16,112},{32,64},{48,16},{64,96},{80,48},{96,0},{112,80},{1... | collective-permute-start | bytes 1572872 | tf_op jit(solution)/shard_map/ppermute | solution.py:391
  24.3 1.9 %collective-permute-start.6 = (bf16[1024,256]{1,0:T(8,128)(2,1)S(1)}, bf16[1024,256]{1,0:T(8,128)(2,1)S(1)}, u32[]{:S(2)}, u32[]{:S(2)}) collective-permute-start(bf16[1024,256]{1,0:T(8,128)(2,1)S(1)} %collective-permute-done.3.rest_1_.rest_3_), channel_id=1, source_target_pairs={{0,16},{16,0},{32,48},{48,32},{64,80},{80,64},{96,112},{112,96},{1... | collective-permute-start | bytes 1572872 | tf_op jit(solution)/shard_map/ppermute | solution.py:391
  24.6 2.4 %collective-permute-start.5 = (bf16[1024,256]{1,0:T(8,128)(2,1)S(1)}, bf16[1024,256]{1,0:T(8,128)(2,1)S(1)}, u32[]{:S(2)}, u32[]{:S(2)}) collective-permute-start(bf16[1024,256]{1,0:T(8,128)(2,1)S(1)} %collective-permute-done.2.rest_0_.rest_5_), channel_id=1, source_target_pairs={{0,16},{16,0},{32,48},{48,32},{64,80},{80,64},{96,112},{112,96},{1... | collective-permute-start | bytes 1572872 | tf_op jit(solution)/shard_map/ppermute | solution.py:391

commit v4 on v3

--- a/solution.py
+++ b/solution.py
@@ -392,13 +392,13 @@
 
     came = send(features, ring)
     beside = send(features, cores)
-    later, beside = lax.optimization_barrier((features, beside))
-    back_came = send(later, back)
     count = queries.shape[0] // space
     weights = (w_query, w_key, w_value, w_out, norm_gain, w_mask)
     folded, items, wv_t, w_out, norm_gain, w_mask, own, mine = project(
         place, count, block_lists.T, queries, *weights, features
     )
+    later, folded = lax.optimization_barrier((features, folded))
+    back_came = send(later, back)
     state = attend(0, items, folded, [own, beside], None, None)
     came, state = lax.optimization_barrier((came, tuple(state)))
     far = send(came, ring)

time: 68.9 us -> 69.3 us (level)
    all_to_all x1, blocking collectives: 17.1 us -> 16.3 us  [shards(): got = lax.all_to_all(partial.reshape(space, count, D + TAIL), 'space', 0, 0)]
  transfers between devices with their start and end apart: 7 -> 7, of which waited for: 4 -> 2; matrix products, arithmetic and copies ran while one was open for 0% -> 0% of each run, Pallas kernels for 18% -> 17%
where the time goes in v4:
time: 69.3 us; the launch traced here: 69.4 us
  blocking collectives  29 us (42%)
  Pallas kernels  25.6 us (37%)
  waiting for transfers between devices  7.99 us (12%)
  starting transfers between devices  6 us (9%)
  between operations  0.71 us (1%)
    all_to_all x1, blocking collectives, shards(): got = lax.all_to_all(partial.reshape(space, count, D + TAIL), 'space', 0, 0)  16.3 us
    pallas_call x3, Pallas kernels, attend(): pl.pallas_call(functools.partial(attend_kernel, phase, sizes, last), out_...  13 us
    all_to_all x1, blocking collectives, shards(): updated = lax.all_to_all(rows, 'space', 0, 0).reshape(queries.shape)  12.6 us
    ppermute x7, waiting for transfers between devices, send(): return lax.ppermute(rows, 'query', pairs)  7.99 us
    pallas_call x1, Pallas kernels, logits(): pl.pallas_call(functools.partial(logits_kernel, pieces), out_shape=(jax.S...  7.05 us
    ppermute x7, starting transfers between devices, send(): return lax.ppermute(rows, 'query', pairs)  6 us
    pallas_call x1, Pallas kernels, project(): pl.pallas_call(project_kernel, out_shape=(jax.ShapeDtypeStruct((blocks, D...  4.91 us
  transfers between devices with their start and end apart: 7, of which 2 were waited for; matrix products, arithmetic and copies ran while one was open for 0% of the time, Pallas kernels for 17%

profile of v4, /device:TPU:0, one launch (start us, length us, event | category | flops | bytes accessed | tf_op | source)
XLA Modules:
  0.0 69.4 jit_solution(11360630506265308757)
XLA Ops:
  0.6 0.1 collective-permute-start.1
  0.7 1.7 %collective-permute-start = (bf16[1024,256]{1,0:T(8,128)(2,1)}, bf16[1024,256]{1,0:T(8,128)(2,1)S(1)}, u32[]{:S(2)}, u32[]{:S(2)}) collective-permute-start(bf16[1024,256]{1,0:T(8,128)(2,1)} %refs_8_.1), channel_id=1, source_target_pairs={{0,32},{16,112},{32,64},{48,16},{64,96},{80,48},{96,0},{112,80},{1... | collective-permute-start | bytes 1572872 | tf_op jit(solution)/shard_map/ppermute | solution.py:391
  2.5 0.1 pad_add_fusion.place_ref
  2.5 4.9 %project.1 = (bf16[8,256,512]{2,1,0:T(8,128)(2,1)S(1)}, s32[8,128]{1,0:T(8,128)S(1)}, bf16[256,256]{1,0:T(8,128)(2,1)S(1)}, bf16[256,256]{1,0:T(8,128)(2,1)S(1)}...) custom-call(s32[2]{0:T(128)S(1)} %pad_add_fusion.place_ref, ...), custom_call_target="tpu_custom_call" | custom-call | flops 603979776 | bytes 3145728 | tf_op jit(solution)/shard_map/project/pallas_call | solution.py:139
  7.4 1.5 %collective-permute-start.3 = (bf16[1024,256]{1,0:T(8,128)(2,1)}, bf16[1024,256]{1,0:T(8,128)(2,1)S(1)}, u32[]{:S(2)}, u32[]{:S(2)}) collective-permute-start(bf16[1024,256]{1,0:T(8,128)(2,1)} %refs_8_.1), channel_id=1, source_target_pairs={{32,0},{112,16},{64,32},{16,48},{96,64},{48,80},{0,96},{80,112},{3... | collective-permute-start | bytes 1572872 | tf_op jit(solution)/shard_map/ppermute | solution.py:391
  8.9 0.0 collective-permute-done.1.rest_1_
  8.9 3.0 %attend_0.1 = (f32[9,256,512]{2,1,0:T(8,128)S(1)}, f32[9,8,512]{2,1,0:T(8,128)S(1)}) custom-call(s32[8,128]{1,0:T(8,128)S(1)} %get-tuple-element.23.items, bf16[8,256,512]{2,1,0:T(8,128)(2,1)S(1)} %get-tuple-element.25.q_ref, bf16[1024,256]{1,0:T(8,128)(2,1)S(1)} %get-tuple-element.26.rest_0_, bf16[1024,256]{1,0:T(8,128)(2,1)S(1)} %collective-permute-done.1.rest_1_), custom_call_target="tpu_custom_call" | custom-call | flops 1000000000 | bytes 4194304 | tf_op jit(solution)/shard_map/attend_0/pallas_call | solution.py:273
  12.0 0.0 collective-permute-done.rest_0_.rest_2_
  12.0 0.1 collective-permute-start.4
  12.1 0.1 collective-permute-start.2
  12.1 6.4 %collective-permute-done.3.rest_1_.rest_3_ = bf16[1024,256]{1,0:T(8,128)(2,1)S(1)} collective-permute-done((bf16[1024,256]{1,0:T(8,128)(2,1)}, bf16[1024,256]{1,0:T(8,128)(2,1)S(1)}, u32[]{:S(2)}, u32[]{:S(2)}) %collective-permute-start.3) | collective-permute-done | bytes 524320 | tf_op jit(solution)/shard_map/ppermute | solution.py:391
  18.6 1.9 %collective-permute-start.6 = (bf16[1024,256]{1,0:T(8,128)(2,1)S(1)}, bf16[1024,256]{1,0:T(8,128)(2,1)S(1)}, u32[]{:S(2)}, u32[]{:S(2)}) collective-permute-start(bf16[1024,256]{1,0:T(8,128)(2,1)S(1)} %collective-permute-done.3.rest_1_.rest_3_), channel_id=1, source_target_pairs={{0,16},{16,0},{32,48},{48,32},{64,80},{80,64},{96,112},{112,96},{1... | collective-permute-start | bytes 1572872 | tf_op jit(solution)/shard_map/ppermute | solution.py:391
  20.5 0.0 collective-permute-done.4.rest_2_.rest_4_
  20.5 4.1 %attend_1.1 = (f32[9,256,512]{2,1,0:T(8,128)S(1)}, f32[9,8,512]{2,1,0:T(8,128)S(1)}) custom-call(s32[8,128]{1,0:T(8,128)S(1)} %get-tuple-element.23.items, bf16[8,256,512]{2,1,0:T(8,128)(2,1)S(1)} %get-tuple-element.25.q_ref, bf16[1024,256]{1,0:T(8,128)(2,1)S(1)} %collective-permute-done.rest_0_.rest_2_, ...), custom_call_target="tpu_custom_call", output_to_operand_aliasing={{0}: (5, {}), {1}: (6, {})} | custom-call | flops 1000000000 | bytes 4194304 | tf_op jit(solution)/shard_map/attend_1/pallas_call | solution.py:273
  24.5 0.0 collective-permute-done.2.rest_0_.rest_5_
  24.5 0.7 collective-permute-start.5
  25.2 0.0 collective-permute-done.6.rest_2_.rest_7_
  25.2 1.5 %collective-permute-done.5.rest_1_.rest_6_ = bf16[1024,256]{1,0:T(8,128)(2,1)S(1)} collective-permute-done((bf16[1024,256]{1,0:T(8,128)(2,1)S(1)}, bf16[1024,256]{1,0:T(8,128)(2,1)S(1)}, u32[]{:S(2)}, u32[]{:S(2)}) %collective-permute-start.5) | collective-permute-done | bytes 524320 | tf_op jit(solution)/shard_map/ppermute | solution.py:391
  26.8 5.9 %attend_2.1 = (f32[9,256,512]{2,1,0:T(8,128)S(1)}, f32[9,8,512]{2,1,0:T(8,128)S(1)}, bf16[512,384]{1,0:T(8,128)(2,1)S(1)}) custom-call(s32[8,128]{1,0:T(8,128)S(1)} %get-tuple-element.23.items, bf16[8,256,512]{2,1,0:T(8,128)(2,1)S(1)} %get-tuple-element.25.q_ref, ...), custom_call_target="tpu_custom_call", output_to_operand_aliasing={{0}: (5, {}), {1}: (6, {})} | custom-call | flops 1000000000 | bytes 4194304 | tf_op jit(solution)/shard_map/attend_2/pallas_call | solution.py:273
  32.7 16.3 %all_to_all.10.got_ref = bf16[16,32,384]{2,1,0:T(8,128)(2,1)S(1)} all-to-all(bf16[16,32,384]{2,1,0:T(8,128)(2,1)S(1)} %bitcast.6), channel_id=1, replica_groups=mesh['query'=8,'space'=16] {'space'}, dimensions={0} | all-to-all | bytes 786432 | tf_op jit(solution)/shard_map/all_to_all | solution.py:411
  49.0 0.6 finish.1
  49.7 12.6 %all_to_all.11 = bf16[16,32,256]{2,1,0:T(8,128)(2,1)S(1)} all-to-all(bf16[16,32,256]{2,1,0:T(8,128)(2,1)S(1)} %finish.1), channel_id=1, replica_groups=mesh['query'=8,'space'=16] {'space'}, dimensions={0} | all-to-all | bytes 524288 | tf_op jit(solution)/shard_map/all_to_all | solution.py:413
  62.3 7.0 %logits.1 = (bf16[512,256]{1,0:T(8,128)(2,1)}, f32[512,8192]{1,0:T(8,128)}) custom-call(s32[2]{0:T(128)S(1)} %pad_add_fusion.place_ref, bf16[512,256]{1,0:T(8,128)(2,1)S(1)} %bitcast.7, bf16[256,256]{1,0:T(8,128)(2,1)S(1)} %get-tuple-element.43.wm, bf16[1024,256]{1,0:T(8,128)(2,1)S(1)} %get-tuple-element.26.rest_0_, ...), custom_call_target="tpu_custom_call" | custom-call | flops 2147483648 | bytes 20971520 | tf_op jit(solution)/shard_map/logits/pallas_call | solution.py:361
Async XLA Ops:
  0.6 8.3 %collective-permute-start.1 = (bf16[1024,256]{1,0:T(8,128)(2,1)}, bf16[1024,256]{1,0:T(8,128)(2,1)S(1)}, u32[]{:S(2)}, u32[]{:S(2)}) collective-permute-start(bf16[1024,256]{1,0:T(8,128)(2,1)} %refs_8_.1), channel_id=1, source_target_pairs={{0,16},{16,0},{32,48},{48,32},{64,80},{80,64},{96,112},{112,96},{1... | collective-permute-start | bytes 1572872 | tf_op jit(solution)/shard_map/ppermute | solution.py:391
  0.7 11.2 %collective-permute-start = (bf16[1024,256]{1,0:T(8,128)(2,1)}, bf16[1024,256]{1,0:T(8,128)(2,1)S(1)}, u32[]{:S(2)}, u32[]{:S(2)}) collective-permute-start(bf16[1024,256]{1,0:T(8,128)(2,1)} %refs_8_.1), channel_id=1, source_target_pairs={{0,32},{16,112},{32,64},{48,16},{64,96},{80,48},{96,0},{112,80},{1... | collective-permute-start | bytes 1572872 | tf_op jit(solution)/shard_map/ppermute | solution.py:391
  7.4 11.1 %collective-permute-start.3 = (bf16[1024,256]{1,0:T(8,128)(2,1)}, bf16[1024,256]{1,0:T(8,128)(2,1)S(1)}, u32[]{:S(2)}, u32[]{:S(2)}) collective-permute-start(bf16[1024,256]{1,0:T(8,128)(2,1)} %refs_8_.1), channel_id=1, source_target_pairs={{32,0},{112,16},{64,32},{16,48},{96,64},{48,80},{0,96},{80,112},{3... | collective-permute-start | bytes 1572872 | tf_op jit(solution)/shard_map/ppermute | solution.py:391
  12.0 8.5 %collective-permute-start.4 = (bf16[1024,256]{1,0:T(8,128)(2,1)S(1)}, bf16[1024,256]{1,0:T(8,128)(2,1)S(1)}, u32[]{:S(2)}, u32[]{:S(2)}) collective-permute-start(bf16[1024,256]{1,0:T(8,128)(2,1)S(1)} %collective-permute-done.rest_0_.rest_2_), channel_id=1, source_target_pairs={{0,16},{16,0},{32,48},{48,32},{64,80},{80,64},{96,112},{112,96},{1... | collective-permute-start | bytes 1572872 | tf_op jit(solution)/shard_map/ppermute | solution.py:391
  12.1 12.5 %collective-permute-start.2 = (bf16[1024,256]{1,0:T(8,128)(2,1)S(1)}, bf16[1024,256]{1,0:T(8,128)(2,1)S(1)}, u32[]{:S(2)}, u32[]{:S(2)}) collective-permute-start(bf16[1024,256]{1,0:T(8,128)(2,1)S(1)} %collective-permute-done.rest_0_.rest_2_), channel_id=1, source_target_pairs={{0,32},{16,112},{32,64},{48,16},{64,96},{80,48},{96,0},{112,80},{1... | collective-permute-start | bytes 1572872 | tf_op jit(solution)/shard_map/ppermute | solution.py:391
  18.6 6.6 %collective-permute-start.6 = (bf16[1024,256]{1,0:T(8,128)(2,1)S(1)}, bf16[1024,256]{1,0:T(8,128)(2,1)S(1)}, u32[]{:S(2)}, u32[]{:S(2)}) collective-permute-start(bf16[1024,256]{1,0:T(8,128)(2,1)S(1)} %collective-permute-done.3.rest_1_.rest_3_), channel_id=1, source_target_pairs={{0,16},{16,0},{32,48},{48,32},{64,80},{80,64},{96,112},{112,96},{1... | collective-permute-start | bytes 1572872 | tf_op jit(solution)/shard_map/ppermute | solution.py:391
  24.5 2.2 %collective-permute-start.5 = (bf16[1024,256]{1,0:T(8,128)(2,1)S(1)}, bf16[1024,256]{1,0:T(8,128)(2,1)S(1)}, u32[]{:S(2)}, u32[]{:S(2)}) collective-permute-start(bf16[1024,256]{1,0:T(8,128)(2,1)S(1)} %collective-permute-done.2.rest_0_.rest_5_), channel_id=1, source_target_pairs={{0,16},{16,0},{32,48},{48,32},{64,80},{80,64},{96,112},{112,96},{1... | collective-permute-start | bytes 1572872 | tf_op jit(solution)/shard_map/ppermute | solution.py:391

commit v5 on v4

--- a/solution.py
+++ b/solution.py
@@ -234,17 +234,20 @@
     for b in range(q_ref.shape[0]):
         diagonal = []
         tail = jnp.zeros((16, WIDE), F32)
-        for c in range(PAIRS):
-            part = slice(c * WIDE, (c + 1) * WIDE)
+        for two in range(PAIRS // 2):
+            part = slice(two * 2 * WIDE, (two + 1) * 2 * WIDE)
             total = stats_ref[b, 1:2, part]
             mean = (acc[b, :, part] * (1.0 / total)).astype(BF16)
-            heads = slice(2 * HD * c, 2 * HD * (c + 1))
-            diagonal.append(jnp.dot(wv_t[heads, :], mean, preferred_element_type=F32))
+            heads = slice(4 * HD * two, 4 * HD * (two + 1))
+            values = jnp.dot(wv_t[heads, :], mean, preferred_element_type=F32)
+            diagonal += [values[: 2 * HD, :WIDE], values[2 * HD :, WIDE:]]
             level = stats_ref[b, 0:1, part] + jnp.log(total) * LOG2E
             for piece in range(3):
                 rounded = level.astype(BF16).astype(F32)
                 level = level - rounded
-                tail = jnp.where(slot == piece * PAIRS + c, rounded, tail)
+                for k in range(2):
+                    at = piece * PAIRS + 2 * two + k
+                    tail = jnp.where(slot == at, rounded[:, k * WIDE : (k + 1) * WIDE], tail)
         turned = jnp.concatenate(diagonal + [tail, tail, empty], axis=0).T
         rows = jnp.where(odd_head == 1, turned[QBLK:], turned[:QBLK])
         out_ref[b * QBLK : (b + 1) * QBLK, :] = rows.astype(BF16)

time: 69.3 us -> 68.6 us (0.990); the launches traced: 69.4 us -> 67.6 us
  Pallas kernels: 25.6 us -> 23 us
  blocking collectives: 29 us -> 29.7 us
    pallas_call x3, Pallas kernels: 13 us -> 10.5 us  [attend(): pl.pallas_call(functools.partial(attend_kernel, phase, sizes, last), out_...]
    all_to_all x1, blocking collectives: 16.3 us -> 17.6 us  [shards(): got = lax.all_to_all(partial.reshape(space, count, D + TAIL), 'space', 0, 0)]
  transfers between devices with their start and end apart: 7 -> 7, of which waited for: 2 -> 3; matrix products, arithmetic and copies ran while one was open for 0% -> 0% of each run, Pallas kernels for 17% -> 17%
where the time goes in v5:
time: 68.6 us; the launch traced here: 67.6 us
  blocking collectives  29.7 us (43%)
  Pallas kernels  23 us (34%)
  waiting for transfers between devices  8.29 us (12%)
  starting transfers between devices  5.88 us (9%)
  between operations  0.7 us (1%)
    all_to_all x1, blocking collectives, shards(): got = lax.all_to_all(partial.reshape(space, count, D + TAIL), 'space', 0, 0)  17.6 us
    all_to_all x1, blocking collectives, shards(): updated = lax.all_to_all(rows, 'space', 0, 0).reshape(queries.shape)  12 us
    pallas_call x3, Pallas kernels, attend(): pl.pallas_call(functools.partial(attend_kernel, phase, sizes, last), out_...  10.5 us
    ppermute x7, waiting for transfers between devices, send(): return lax.ppermute(rows, 'query', pairs)  8.29 us
    pallas_call x1, Pallas kernels, logits(): pl.pallas_call(functools.partial(logits_kernel, pieces), out_shape=(jax.S...  7.05 us
    ppermute x7, starting transfers between devices, send(): return lax.ppermute(rows, 'query', pairs)  5.88 us
    pallas_call x1, Pallas kernels, project(): pl.pallas_call(project_kernel, out_shape=(jax.ShapeDtypeStruct((blocks, D...  4.82 us
  transfers between devices with their start and end apart: 7, of which 3 were waited for; matrix products, arithmetic and copies ran while one was open for 0% of the time, Pallas kernels for 17%

profile of v5, /device:TPU:0, one launch (start us, length us, event | category | flops | bytes accessed | tf_op | source)
XLA Modules:
  0.0 67.6 jit_solution(13944987602858928424)
XLA Ops:
  0.6 0.1 collective-permute-start.1
  0.7 1.7 %collective-permute-start = (bf16[1024,256]{1,0:T(8,128)(2,1)}, bf16[1024,256]{1,0:T(8,128)(2,1)S(1)}, u32[]{:S(2)}, u32[]{:S(2)}) collective-permute-start(bf16[1024,256]{1,0:T(8,128)(2,1)} %refs_8_.1), channel_id=1, source_target_pairs={{0,32},{16,112},{32,64},{48,16},{64,96},{80,48},{96,0},{112,80},{1... | collective-permute-start | bytes 1572872 | tf_op jit(solution)/shard_map/ppermute | solution.py:394
  2.5 0.1 pad_add_fusion.place_ref
  2.5 4.8 %project.1 = (bf16[8,256,512]{2,1,0:T(8,128)(2,1)S(1)}, s32[8,128]{1,0:T(8,128)S(1)}, bf16[256,256]{1,0:T(8,128)(2,1)S(1)}, bf16[256,256]{1,0:T(8,128)(2,1)S(1)}...) custom-call(s32[2]{0:T(128)S(1)} %pad_add_fusion.place_ref, ...), custom_call_target="tpu_custom_call" | custom-call | flops 603979776 | bytes 3145728 | tf_op jit(solution)/shard_map/project/pallas_call | solution.py:139
  7.4 1.7 %collective-permute-start.3 = (bf16[1024,256]{1,0:T(8,128)(2,1)}, bf16[1024,256]{1,0:T(8,128)(2,1)S(1)}, u32[]{:S(2)}, u32[]{:S(2)}) collective-permute-start(bf16[1024,256]{1,0:T(8,128)(2,1)} %refs_8_.1), channel_id=1, source_target_pairs={{32,0},{112,16},{64,32},{16,48},{96,64},{48,80},{0,96},{80,112},{3... | collective-permute-start | bytes 1572872 | tf_op jit(solution)/shard_map/ppermute | solution.py:394
  9.0 0.0 collective-permute-done.1.rest_1_
  9.0 3.0 %attend_0.1 = (f32[9,256,512]{2,1,0:T(8,128)S(1)}, f32[9,8,512]{2,1,0:T(8,128)S(1)}) custom-call(s32[8,128]{1,0:T(8,128)S(1)} %get-tuple-element.23.items, bf16[8,256,512]{2,1,0:T(8,128)(2,1)S(1)} %get-tuple-element.25.q_ref, bf16[1024,256]{1,0:T(8,128)(2,1)S(1)} %get-tuple-element.26.rest_0_, bf16[1024,256]{1,0:T(8,128)(2,1)S(1)} %collective-permute-done.1.rest_1_), custom_call_target="tpu_custom_call" | custom-call | flops 1000000000 | bytes 4194304 | tf_op jit(solution)/shard_map/attend_0/pallas_call | solution.py:276
  12.1 0.0 collective-permute-done.rest_0_.rest_2_
  12.1 0.1 collective-permute-start.4
  12.2 0.1 collective-permute-start.2
  12.2 6.1 %collective-permute-done.3.rest_1_.rest_3_ = bf16[1024,256]{1,0:T(8,128)(2,1)S(1)} collective-permute-done((bf16[1024,256]{1,0:T(8,128)(2,1)}, bf16[1024,256]{1,0:T(8,128)(2,1)S(1)}, u32[]{:S(2)}, u32[]{:S(2)}) %collective-permute-start.3) | collective-permute-done | bytes 524320 | tf_op jit(solution)/shard_map/ppermute | solution.py:394
  18.3 2.0 %collective-permute-start.6 = (bf16[1024,256]{1,0:T(8,128)(2,1)S(1)}, bf16[1024,256]{1,0:T(8,128)(2,1)S(1)}, u32[]{:S(2)}, u32[]{:S(2)}) collective-permute-start(bf16[1024,256]{1,0:T(8,128)(2,1)S(1)} %collective-permute-done.3.rest_1_.rest_3_), channel_id=1, source_target_pairs={{0,16},{16,0},{32,48},{48,32},{64,80},{80,64},{96,112},{112,96},{1... | collective-permute-start | bytes 1572872 | tf_op jit(solution)/shard_map/ppermute | solution.py:394
  20.3 0.0 collective-permute-done.4.rest_2_.rest_4_
  20.3 3.4 %attend_1.1 = (f32[9,256,512]{2,1,0:T(8,128)S(1)}, f32[9,8,512]{2,1,0:T(8,128)S(1)}) custom-call(s32[8,128]{1,0:T(8,128)S(1)} %get-tuple-element.23.items, bf16[8,256,512]{2,1,0:T(8,128)(2,1)S(1)} %get-tuple-element.25.q_ref, bf16[1024,256]{1,0:T(8,128)(2,1)S(1)} %collective-permute-done.rest_0_.rest_2_, ...), custom_call_target="tpu_custom_call", output_to_operand_aliasing={{0}: (5, {}), {1}: (6, {})} | custom-call | flops 1000000000 | bytes 4194304 | tf_op jit(solution)/shard_map/attend_1/pallas_call | solution.py:276
  23.8 0.5 collective-permute-done.2.rest_0_.rest_5_
  24.3 0.2 collective-permute-start.5
  24.5 0.0 collective-permute-done.6.rest_2_.rest_7_
  24.5 1.7 %collective-permute-done.5.rest_1_.rest_6_ = bf16[1024,256]{1,0:T(8,128)(2,1)S(1)} collective-permute-done((bf16[1024,256]{1,0:T(8,128)(2,1)S(1)}, bf16[1024,256]{1,0:T(8,128)(2,1)S(1)}, u32[]{:S(2)}, u32[]{:S(2)}) %collective-permute-start.5) | collective-permute-done | bytes 524320 | tf_op jit(solution)/shard_map/ppermute | solution.py:394
  26.2 4.1 %attend_2.1 = (f32[9,256,512]{2,1,0:T(8,128)S(1)}, f32[9,8,512]{2,1,0:T(8,128)S(1)}, bf16[512,384]{1,0:T(8,128)(2,1)S(1)}) custom-call(s32[8,128]{1,0:T(8,128)S(1)} %get-tuple-element.23.items, bf16[8,256,512]{2,1,0:T(8,128)(2,1)S(1)} %get-tuple-element.25.q_ref, ...), custom_call_target="tpu_custom_call", output_to_operand_aliasing={{0}: (5, {}), {1}: (6, {})} | custom-call | flops 1000000000 | bytes 4194304 | tf_op jit(solution)/shard_map/attend_2/pallas_call | solution.py:276
  30.3 17.6 %all_to_all.10.got_ref = bf16[16,32,384]{2,1,0:T(8,128)(2,1)S(1)} all-to-all(bf16[16,32,384]{2,1,0:T(8,128)(2,1)S(1)} %bitcast.6), channel_id=1, replica_groups=mesh['query'=8,'space'=16] {'space'}, dimensions={0} | all-to-all | bytes 786432 | tf_op jit(solution)/shard_map/all_to_all | solution.py:414
  47.9 0.6 finish.1
  48.5 12.0 %all_to_all.11 = bf16[16,32,256]{2,1,0:T(8,128)(2,1)S(1)} all-to-all(bf16[16,32,256]{2,1,0:T(8,128)(2,1)S(1)} %finish.1), channel_id=1, replica_groups=mesh['query'=8,'space'=16] {'space'}, dimensions={0} | all-to-all | bytes 524288 | tf_op jit(solution)/shard_map/all_to_all | solution.py:416
  60.6 7.1 %logits.1 = (bf16[512,256]{1,0:T(8,128)(2,1)}, f32[512,8192]{1,0:T(8,128)}) custom-call(s32[2]{0:T(128)S(1)} %pad_add_fusion.place_ref, bf16[512,256]{1,0:T(8,128)(2,1)S(1)} %bitcast.7, bf16[256,256]{1,0:T(8,128)(2,1)S(1)} %get-tuple-element.43.wm, bf16[1024,256]{1,0:T(8,128)(2,1)S(1)} %get-tuple-element.26.rest_0_, ...), custom_call_target="tpu_custom_call" | custom-call | flops 2147483648 | bytes 20971520 | tf_op jit(solution)/shard_map/logits/pallas_call | solution.py:364
Async XLA Ops:
  0.6 8.4 %collective-permute-start.1 = (bf16[1024,256]{1,0:T(8,128)(2,1)}, bf16[1024,256]{1,0:T(8,128)(2,1)S(1)}, u32[]{:S(2)}, u32[]{:S(2)}) collective-permute-start(bf16[1024,256]{1,0:T(8,128)(2,1)} %refs_8_.1), channel_id=1, source_target_pairs={{0,16},{16,0},{32,48},{48,32},{64,80},{80,64},{96,112},{112,96},{1... | collective-permute-start | bytes 1572872 | tf_op jit(solution)/shard_map/ppermute | solution.py:394
  0.7 11.3 %collective-permute-start = (bf16[1024,256]{1,0:T(8,128)(2,1)}, bf16[1024,256]{1,0:T(8,128)(2,1)S(1)}, u32[]{:S(2)}, u32[]{:S(2)}) collective-permute-start(bf16[1024,256]{1,0:T(8,128)(2,1)} %refs_8_.1), channel_id=1, source_target_pairs={{0,32},{16,112},{32,64},{48,16},{64,96},{80,48},{96,0},{112,80},{1... | collective-permute-start | bytes 1572872 | tf_op jit(solution)/shard_map/ppermute | solution.py:394
  7.4 11.0 %collective-permute-start.3 = (bf16[1024,256]{1,0:T(8,128)(2,1)}, bf16[1024,256]{1,0:T(8,128)(2,1)S(1)}, u32[]{:S(2)}, u32[]{:S(2)}) collective-permute-start(bf16[1024,256]{1,0:T(8,128)(2,1)} %refs_8_.1), channel_id=1, source_target_pairs={{32,0},{112,16},{64,32},{16,48},{96,64},{48,80},{0,96},{80,112},{3... | collective-permute-start | bytes 1572872 | tf_op jit(solution)/shard_map/ppermute | solution.py:394
  12.1 8.3 %collective-permute-start.4 = (bf16[1024,256]{1,0:T(8,128)(2,1)S(1)}, bf16[1024,256]{1,0:T(8,128)(2,1)S(1)}, u32[]{:S(2)}, u32[]{:S(2)}) collective-permute-start(bf16[1024,256]{1,0:T(8,128)(2,1)S(1)} %collective-permute-done.rest_0_.rest_2_), channel_id=1, source_target_pairs={{0,16},{16,0},{32,48},{48,32},{64,80},{80,64},{96,112},{112,96},{1... | collective-permute-start | bytes 1572872 | tf_op jit(solution)/shard_map/ppermute | solution.py:394
  12.2 12.1 %collective-permute-start.2 = (bf16[1024,256]{1,0:T(8,128)(2,1)S(1)}, bf16[1024,256]{1,0:T(8,128)(2,1)S(1)}, u32[]{:S(2)}, u32[]{:S(2)}) collective-permute-start(bf16[1024,256]{1,0:T(8,128)(2,1)S(1)} %collective-permute-done.rest_0_.rest_2_), channel_id=1, source_target_pairs={{0,32},{16,112},{32,64},{48,16},{64,96},{80,48},{96,0},{112,80},{1... | collective-permute-start | bytes 1572872 | tf_op jit(solution)/shard_map/ppermute | solution.py:394
  18.3 6.2 %collective-permute-start.6 = (bf16[1024,256]{1,0:T(8,128)(2,1)S(1)}, bf16[1024,256]{1,0:T(8,128)(2,1)S(1)}, u32[]{:S(2)}, u32[]{:S(2)}) collective-permute-start(bf16[1024,256]{1,0:T(8,128)(2,1)S(1)} %collective-permute-done.3.rest_1_.rest_3_), channel_id=1, source_target_pairs={{0,16},{16,0},{32,48},{48,32},{64,80},{80,64},{96,112},{112,96},{1... | collective-permute-start | bytes 1572872 | tf_op jit(solution)/shard_map/ppermute | solution.py:394
  24.3 1.9 %collective-permute-start.5 = (bf16[1024,256]{1,0:T(8,128)(2,1)S(1)}, bf16[1024,256]{1,0:T(8,128)(2,1)S(1)}, u32[]{:S(2)}, u32[]{:S(2)}) collective-permute-start(bf16[1024,256]{1,0:T(8,128)(2,1)S(1)} %collective-permute-done.2.rest_0_.rest_5_), channel_id=1, source_target_pairs={{0,16},{16,0},{32,48},{48,32},{64,80},{80,64},{96,112},{112,96},{1... | collective-permute-start | bytes 1572872 | tf_op jit(solution)/shard_map/ppermute | solution.py:394

commit v6 on v5

--- a/solution.py
+++ b/solution.py
@@ -23,7 +23,7 @@
 CHIPS = 4
 OWN_BLOCKS = 8
 SHARD_BLOCKS = 2 * CHIPS * OWN_BLOCKS
-PHASES = 3
+PHASES = 4
 WIDTH = 20
 LAST = 127
 COUNTS = PHASES * WIDTH
@@ -52,8 +52,10 @@
     toward = jnp.where(core == 0, CHIPS - 1, 1)
     near = (ahead == 1) | (ahead == CHIPS - 1)
     late = near & (ahead == toward) & (other == 1)
-    position = jnp.where(near & (ahead != toward), 1 + other, jnp.where(near, 2 * other, other)) * OWN_BLOCKS + inside
-    phase = jnp.where(ahead == 0, 0, jnp.where(near & ~late, 1, 2))
+    away = jnp.where(near & (ahead != toward), 1 + other, 0)
+    position = jnp.where(late, 1, away) * OWN_BLOCKS + inside
+    position = jnp.where(ahead == 0, other * OWN_BLOCKS + inside, position)
+    phase = jnp.where(ahead == 0, 0, jnp.where(near & ~late, 1, jnp.where(late | (other == 0), 2, 3)))
     phase = jnp.where(lax.div(lists, SHARD_BLOCKS) == place_ref[1], phase, -1)
     width = lists.shape[0]
     row = lax.broadcasted_iota(jnp.int32, (width, width), 0)
@@ -408,14 +410,15 @@
     near = [came, back_came, send(came, cores)]
     state = attend(1, items, folded, near, state, None)
     far, state = lax.optimization_barrier((far, tuple(state)))
-    far = [far, send(far, cores), send(back_came, cores)]
-    partial = attend(2, items, folded, far, state, wv_t)[2]
+    final = [far, send(back_came, cores), send(far, cores)]
+    state = attend(2, items, folded, final[:2], state, None)
+    partial = attend(3, items, folded, final[2:], state, wv_t)[2]
 
     got = lax.all_to_all(partial.reshape(space, count, D + TAIL), "space", 0, 0)
     rows = finish(got, mine, w_out, norm_gain)
     updated = lax.all_to_all(rows, "space", 0, 0).reshape(queries.shape)
-    pieces = [(0, False), (0, True), (1, False), (-1, False), (-1, True), (2, False), (2, True), (1, True)]
-    return logits(place, updated, w_mask, pieces, [own, beside, *near, *far])
+    pieces = [(0, False), (0, True), (1, False), (-1, False), (-1, True), (2, False), (1, True), (2, True)]
+    return logits(place, updated, w_mask, pieces, [own, beside, *near, *final])
 
 
 def solution(mesh):

time: 68.6 us -> 68.3 us (level); the launches traced: 67.6 us -> 68.1 us
  Pallas kernels: 23 us -> 25.9 us
  waiting for transfers between devices: 8.29 us -> 5.68 us
    pallas_call x3 -> x4, Pallas kernels: 10.5 us -> 13.2 us  [attend(): pl.pallas_call(functools.partial(attend_kernel, phase, sizes, last), out_...]
    ppermute x7, waiting for transfers between devices: 8.29 us -> 5.68 us  [send(): return lax.ppermute(rows, 'query', pairs)]
  transfers between devices with their start and end apart: 7 -> 7, of which waited for: 3 -> 2; matrix products, arithmetic and copies ran while one was open for 0% -> 0% of each run, Pallas kernels for 17% -> 22%
where the time goes in v6:
time: 68.3 us; the launch traced here: 68.1 us
  blocking collectives  29.8 us (44%)
  Pallas kernels  25.9 us (38%)
  starting transfers between devices  5.8 us (8%)
  waiting for transfers between devices  5.68 us (8%)
  between operations  0.71 us (1%)
    all_to_all x1, blocking collectives, shards(): got = lax.all_to_all(partial.reshape(space, count, D + TAIL), 'space', 0, 0)  17.8 us
    pallas_call x4, Pallas kernels, attend(): pl.pallas_call(functools.partial(attend_kernel, phase, sizes, last), out_...  13.2 us
    all_to_all x1, blocking collectives, shards(): updated = lax.all_to_all(rows, 'space', 0, 0).reshape(queries.shape)  12 us
    pallas_call x1, Pallas kernels, logits(): pl.pallas_call(functools.partial(logits_kernel, pieces), out_shape=(jax.S...  7.05 us
    ppermute x7, starting transfers between devices, send(): return lax.ppermute(rows, 'query', pairs)  5.8 us
    ppermute x7, waiting for transfers between devices, send(): return lax.ppermute(rows, 'query', pairs)  5.68 us
    pallas_call x1, Pallas kernels, project(): pl.pallas_call(project_kernel, out_shape=(jax.ShapeDtypeStruct((blocks, D...  5.04 us
  transfers between devices with their start and end apart: 7, of which 2 were waited for; matrix products, arithmetic and copies ran while one was open for 0% of the time, Pallas kernels for 22%

profile of v6, /device:TPU:0, one launch (start us, length us, event | category | flops | bytes accessed | tf_op | source)
XLA Modules:
  0.0 68.1 jit_solution(15952161421926782816)
XLA Ops:
  0.6 0.1 collective-permute-start.1
  0.7 1.7 %collective-permute-start = (bf16[1024,256]{1,0:T(8,128)(2,1)}, bf16[1024,256]{1,0:T(8,128)(2,1)S(1)}, u32[]{:S(2)}, u32[]{:S(2)}) collective-permute-start(bf16[1024,256]{1,0:T(8,128)(2,1)} %refs_8_.1), channel_id=1, source_target_pairs={{0,32},{16,112},{32,64},{48,16},{64,96},{80,48},{96,0},{112,80},{1... | collective-permute-start | bytes 1572872 | tf_op jit(solution)/shard_map/ppermute | solution.py:396
  2.5 0.1 pad_add_fusion.place_ref
  2.5 5.0 %project.1 = (bf16[8,256,512]{2,1,0:T(8,128)(2,1)S(1)}, s32[8,128]{1,0:T(8,128)S(1)}, bf16[256,256]{1,0:T(8,128)(2,1)S(1)}, bf16[256,256]{1,0:T(8,128)(2,1)S(1)}...) custom-call(s32[2]{0:T(128)S(1)} %pad_add_fusion.place_ref, ...), custom_call_target="tpu_custom_call" | custom-call | flops 603979776 | bytes 3145728 | tf_op jit(solution)/shard_map/project/pallas_call | solution.py:141
  7.6 1.5 %collective-permute-start.3 = (bf16[1024,256]{1,0:T(8,128)(2,1)}, bf16[1024,256]{1,0:T(8,128)(2,1)S(1)}, u32[]{:S(2)}, u32[]{:S(2)}) collective-permute-start(bf16[1024,256]{1,0:T(8,128)(2,1)} %refs_8_.1), channel_id=1, source_target_pairs={{32,0},{112,16},{64,32},{16,48},{96,64},{48,80},{0,96},{80,112},{3... | collective-permute-start | bytes 1572872 | tf_op jit(solution)/shard_map/ppermute | solution.py:396
  9.1 0.0 collective-permute-done.1.rest_1_
  9.1 3.7 %attend_0.1 = (f32[9,256,512]{2,1,0:T(8,128)S(1)}, f32[9,8,512]{2,1,0:T(8,128)S(1)}) custom-call(s32[8,128]{1,0:T(8,128)S(1)} %get-tuple-element.25.items, bf16[8,256,512]{2,1,0:T(8,128)(2,1)S(1)} %get-tuple-element.27.q_ref, bf16[1024,256]{1,0:T(8,128)(2,1)S(1)} %get-tuple-element.28.rest_0_, bf16[1024,256]{1,0:T(8,128)(2,1)S(1)} %collective-permute-done.1.rest_1_), custom_call_target="tpu_custom_call" | custom-call | flops 1000000000 | bytes 4194304 | tf_op jit(solution)/shard_map/attend_0/pallas_call | solution.py:278
  12.7 0.0 collective-permute-done.rest_0_.rest_2_
  12.7 0.1 collective-permute-start.4
  12.8 0.7 collective-permute-start.2
  13.5 4.6 %collective-permute-done.3.rest_1_.rest_3_ = bf16[1024,256]{1,0:T(8,128)(2,1)S(1)} collective-permute-done((bf16[1024,256]{1,0:T(8,128)(2,1)}, bf16[1024,256]{1,0:T(8,128)(2,1)S(1)}, u32[]{:S(2)}, u32[]{:S(2)}) %collective-permute-start.3) | collective-permute-done | bytes 524320 | tf_op jit(solution)/shard_map/ppermute | solution.py:396
  18.1 1.7 %collective-permute-start.6 = (bf16[1024,256]{1,0:T(8,128)(2,1)S(1)}, bf16[1024,256]{1,0:T(8,128)(2,1)S(1)}, u32[]{:S(2)}, u32[]{:S(2)}) collective-permute-start(bf16[1024,256]{1,0:T(8,128)(2,1)S(1)} %collective-permute-done.3.rest_1_.rest_3_), channel_id=1, source_target_pairs={{0,16},{16,0},{32,48},{48,32},{64,80},{80,64},{96,112},{112,96},{1... | collective-permute-start | bytes 1572872 | tf_op jit(solution)/shard_map/ppermute | solution.py:396
  19.8 0.0 collective-permute-done.4.rest_2_.rest_4_
  19.8 3.4 %attend_1.1 = (f32[9,256,512]{2,1,0:T(8,128)S(1)}, f32[9,8,512]{2,1,0:T(8,128)S(1)}) custom-call(s32[8,128]{1,0:T(8,128)S(1)} %get-tuple-element.25.items, bf16[8,256,512]{2,1,0:T(8,128)(2,1)S(1)} %get-tuple-element.27.q_ref, bf16[1024,256]{1,0:T(8,128)(2,1)S(1)} %collective-permute-done.rest_0_.rest_2_, ...), custom_call_target="tpu_custom_call", output_to_operand_aliasing={{0}: (5, {}), {1}: (6, {})} | custom-call | flops 1000000000 | bytes 4194304 | tf_op jit(solution)/shard_map/attend_1/pallas_call | solution.py:278
  23.2 1.1 %collective-permute-done.2.rest_0_.rest_5_ = bf16[1024,256]{1,0:T(8,128)(2,1)S(1)} collective-permute-done((bf16[1024,256]{1,0:T(8,128)(2,1)S(1)}, bf16[1024,256]{1,0:T(8,128)(2,1)S(1)}, u32[]{:S(2)}, u32[]{:S(2)}) %collective-permute-start.2) | collective-permute-done | bytes 524320 | tf_op jit(solution)/shard_map/ppermute | solution.py:396
  24.3 0.0 collective-permute-start.5
  24.3 0.0 collective-permute-done.6.rest_1_.rest_6_
  24.3 2.8 %attend_2.1 = (f32[9,256,512]{2,1,0:T(8,128)S(1)}, f32[9,8,512]{2,1,0:T(8,128)S(1)}) custom-call(s32[8,128]{1,0:T(8,128)S(1)} %get-tuple-element.25.items, bf16[8,256,512]{2,1,0:T(8,128)(2,1)S(1)} %get-tuple-element.27.q_ref, bf16[1024,256]{1,0:T(8,128)(2,1)S(1)} %collective-permute-done.2.rest_0_.rest_5_, ...), custom_call_target="tpu_custom_call", output_to_operand_aliasing={{0}: (4, {}), {1}: (5, {})} | custom-call | flops 1000000000 | bytes 4194304 | tf_op jit(solution)/shard_map/attend_2/pallas_call | solution.py:278
  27.1 0.0 collective-permute-done.5.rest_0_.rest_7_
  27.1 3.4 %attend_3.1 = (f32[9,256,512]{2,1,0:T(8,128)S(1)}, f32[9,8,512]{2,1,0:T(8,128)S(1)}, bf16[512,384]{1,0:T(8,128)(2,1)S(1)}) custom-call(s32[8,128]{1,0:T(8,128)S(1)} %get-tuple-element.25.items, bf16[8,256,512]{2,1,0:T(8,128)(2,1)S(1)} %get-tuple-element.27.q_ref, ...), custom_call_target="tpu_custom_call", output_to_operand_aliasing={{0}: (3, {}), {1}: (4, {})} | custom-call | flops 1000000000 | bytes 4194304 | tf_op jit(solution)/shard_map/attend_3/pallas_call | solution.py:278
  30.5 17.8 %all_to_all.10.got_ref = bf16[16,32,384]{2,1,0:T(8,128)(2,1)S(1)} all-to-all(bf16[16,32,384]{2,1,0:T(8,128)(2,1)S(1)} %bitcast.6), channel_id=1, replica_groups=mesh['query'=8,'space'=16] {'space'}, dimensions={0} | all-to-all | bytes 786432 | tf_op jit(solution)/shard_map/all_to_all | solution.py:417
  48.3 0.6 finish.1
  49.0 12.0 %all_to_all.11 = bf16[16,32,256]{2,1,0:T(8,128)(2,1)S(1)} all-to-all(bf16[16,32,256]{2,1,0:T(8,128)(2,1)S(1)} %finish.1), channel_id=1, replica_groups=mesh['query'=8,'space'=16] {'space'}, dimensions={0} | all-to-all | bytes 524288 | tf_op jit(solution)/shard_map/all_to_all | solution.py:419
  61.0 7.1 %logits.1 = (bf16[512,256]{1,0:T(8,128)(2,1)}, f32[512,8192]{1,0:T(8,128)}) custom-call(s32[2]{0:T(128)S(1)} %pad_add_fusion.place_ref, bf16[512,256]{1,0:T(8,128)(2,1)S(1)} %bitcast.7, bf16[256,256]{1,0:T(8,128)(2,1)S(1)} %get-tuple-element.47.wm, bf16[1024,256]{1,0:T(8,128)(2,1)S(1)} %get-tuple-element.28.rest_0_, ...), custom_call_target="tpu_custom_call" | custom-call | flops 2147483648 | bytes 20971520 | tf_op jit(solution)/shard_map/logits/pallas_call | solution.py:366
Async XLA Ops:
  0.6 8.4 %collective-permute-start.1 = (bf16[1024,256]{1,0:T(8,128)(2,1)}, bf16[1024,256]{1,0:T(8,128)(2,1)S(1)}, u32[]{:S(2)}, u32[]{:S(2)}) collective-permute-start(bf16[1024,256]{1,0:T(8,128)(2,1)} %refs_8_.1), channel_id=1, source_target_pairs={{0,16},{16,0},{32,48},{48,32},{64,80},{80,64},{96,112},{112,96},{1... | collective-permute-start | bytes 1572872 | tf_op jit(solution)/shard_map/ppermute | solution.py:396
  0.7 12.0 %collective-permute-start = (bf16[1024,256]{1,0:T(8,128)(2,1)}, bf16[1024,256]{1,0:T(8,128)(2,1)S(1)}, u32[]{:S(2)}, u32[]{:S(2)}) collective-permute-start(bf16[1024,256]{1,0:T(8,128)(2,1)} %refs_8_.1), channel_id=1, source_target_pairs={{0,32},{16,112},{32,64},{48,16},{64,96},{80,48},{96,0},{112,80},{1... | collective-permute-start | bytes 1572872 | tf_op jit(solution)/shard_map/ppermute | solution.py:396
  7.6 10.5 %collective-permute-start.3 = (bf16[1024,256]{1,0:T(8,128)(2,1)}, bf16[1024,256]{1,0:T(8,128)(2,1)S(1)}, u32[]{:S(2)}, u32[]{:S(2)}) collective-permute-start(bf16[1024,256]{1,0:T(8,128)(2,1)} %refs_8_.1), channel_id=1, source_target_pairs={{32,0},{112,16},{64,32},{16,48},{96,64},{48,80},{0,96},{80,112},{3... | collective-permute-start | bytes 1572872 | tf_op jit(solution)/shard_map/ppermute | solution.py:396
  12.7 7.1 %collective-permute-start.4 = (bf16[1024,256]{1,0:T(8,128)(2,1)S(1)}, bf16[1024,256]{1,0:T(8,128)(2,1)S(1)}, u32[]{:S(2)}, u32[]{:S(2)}) collective-permute-start(bf16[1024,256]{1,0:T(8,128)(2,1)S(1)} %collective-permute-done.rest_0_.rest_2_), channel_id=1, source_target_pairs={{0,16},{16,0},{32,48},{48,32},{64,80},{80,64},{96,112},{112,96},{1... | collective-permute-start | bytes 1572872 | tf_op jit(solution)/shard_map/ppermute | solution.py:396
  12.8 11.5 %collective-permute-start.2 = (bf16[1024,256]{1,0:T(8,128)(2,1)S(1)}, bf16[1024,256]{1,0:T(8,128)(2,1)S(1)}, u32[]{:S(2)}, u32[]{:S(2)}) collective-permute-start(bf16[1024,256]{1,0:T(8,128)(2,1)S(1)} %collective-permute-done.rest_0_.rest_2_), channel_id=1, source_target_pairs={{0,32},{16,112},{32,64},{48,16},{64,96},{80,48},{96,0},{112,80},{1... | collective-permute-start | bytes 1572872 | tf_op jit(solution)/shard_map/ppermute | solution.py:396
  18.1 6.3 %collective-permute-start.6 = (bf16[1024,256]{1,0:T(8,128)(2,1)S(1)}, bf16[1024,256]{1,0:T(8,128)(2,1)S(1)}, u32[]{:S(2)}, u32[]{:S(2)}) collective-permute-start(bf16[1024,256]{1,0:T(8,128)(2,1)S(1)} %collective-permute-done.3.rest_1_.rest_3_), channel_id=1, source_target_pairs={{0,16},{16,0},{32,48},{48,32},{64,80},{80,64},{96,112},{112,96},{1... | collective-permute-start | bytes 1572872 | tf_op jit(solution)/shard_map/ppermute | solution.py:396
  24.3 2.8 %collective-permute-start.5 = (bf16[1024,256]{1,0:T(8,128)(2,1)S(1)}, bf16[1024,256]{1,0:T(8,128)(2,1)S(1)}, u32[]{:S(2)}, u32[]{:S(2)}) collective-permute-start(bf16[1024,256]{1,0:T(8,128)(2,1)S(1)} %collective-permute-done.2.rest_0_.rest_5_), channel_id=1, source_target_pairs={{0,16},{16,0},{32,48},{48,32},{64,80},{80,64},{96,112},{112,96},{1... | collective-permute-start | bytes 1572872 | tf_op jit(solution)/shard_map/ppermute | solution.py:396

commit v7 on v6

--- a/solution.py
+++ b/solution.py
@@ -210,9 +210,12 @@
     else:
         acc, stats_ref, feats, even, odd = rest
     held = 0
-    for size, ref in zip(sizes, piece_refs):
-        feats[held : held + size, :] = ref[...]
-        held += size
+    if count == 1:
+        feats = piece_refs[0]
+    else:
+        for size, ref in zip(sizes, piece_refs):
+            feats[held : held + size, :] = ref[...]
+            held += size
     if phase == 0:
         acc[...] = jnp.zeros(acc.shape, F32)
         stats_ref[:, 0:1, :] = jnp.full((acc.shape[0], 1, H * QBLK), -jnp.inf, F32)
@@ -322,7 +325,7 @@
 
 
 STEP = 512
-SLOTS = 4
+SLOTS = 8
 
 
 def piece_row(place_ref, piece):

time: 68.3 us -> 67.9 us (level)
  Pallas kernels: 25.9 us -> 27.1 us
  waiting for transfers between devices: 5.68 us -> 4.58 us
    pallas_call x4, Pallas kernels: 13.2 us -> 14.4 us  [attend(): pl.pallas_call(functools.partial(attend_kernel, phase, sizes, last), out_...]
    ppermute x7, waiting for transfers between devices: 5.68 us -> 4.58 us  [send(): return lax.ppermute(rows, 'query', pairs)]
  transfers between devices with their start and end apart: 7 -> 7, of which waited for: 2 -> 1; matrix products, arithmetic and copies ran while one was open for 0% -> 0% of each run, Pallas kernels for 22% -> 24%
where the time goes in v7:
time: 67.9 us; the launch traced here: 67.7 us
  blocking collectives  29.3 us (43%)
  Pallas kernels  27.1 us (40%)
  starting transfers between devices  5.98 us (9%)
  waiting for transfers between devices  4.58 us (7%)
  between operations  0.73 us (1%)
    all_to_all x1, blocking collectives, shards(): got = lax.all_to_all(partial.reshape(space, count, D + TAIL), 'space', 0, 0)  17.5 us
    pallas_call x4, Pallas kernels, attend(): pl.pallas_call(functools.partial(attend_kernel, phase, sizes, last), out_...  14.4 us
    all_to_all x1, blocking collectives, shards(): updated = lax.all_to_all(rows, 'space', 0, 0).reshape(queries.shape)  11.8 us
    pallas_call x1, Pallas kernels, logits(): pl.pallas_call(functools.partial(logits_kernel, pieces), out_shape=(jax.S...  6.95 us
    ppermute x7, starting transfers between devices, send(): return lax.ppermute(rows, 'query', pairs)  5.98 us
    pallas_call x1, Pallas kernels, project(): pl.pallas_call(project_kernel, out_shape=(jax.ShapeDtypeStruct((blocks, D...  5.06 us
    ppermute x7, waiting for transfers between devices, send(): return lax.ppermute(rows, 'query', pairs)  4.58 us
  transfers between devices with their start and end apart: 7, of which 1 were waited for; matrix products, arithmetic and copies ran while one was open for 0% of the time, Pallas kernels for 24%

profile of v7, /device:TPU:0, one launch (start us, length us, event | category | flops | bytes accessed | tf_op | source)
XLA Modules:
  0.0 67.7 jit_solution(2374030816032902337)
XLA Ops:
  0.6 0.1 collective-permute-start.1
  0.7 1.7 %collective-permute-start = (bf16[1024,256]{1,0:T(8,128)(2,1)}, bf16[1024,256]{1,0:T(8,128)(2,1)S(1)}, u32[]{:S(2)}, u32[]{:S(2)}) collective-permute-start(bf16[1024,256]{1,0:T(8,128)(2,1)} %refs_8_.1), channel_id=1, source_target_pairs={{0,32},{16,112},{32,64},{48,16},{64,96},{80,48},{96,0},{112,80},{1... | collective-permute-start | bytes 1572872 | tf_op jit(solution)/shard_map/ppermute | solution.py:399
  2.5 0.1 pad_add_fusion.place_ref
  2.5 5.1 %project.1 = (bf16[8,256,512]{2,1,0:T(8,128)(2,1)S(1)}, s32[8,128]{1,0:T(8,128)S(1)}, bf16[256,256]{1,0:T(8,128)(2,1)S(1)}, bf16[256,256]{1,0:T(8,128)(2,1)S(1)}...) custom-call(s32[2]{0:T(128)S(1)} %pad_add_fusion.place_ref, ...), custom_call_target="tpu_custom_call" | custom-call | flops 603979776 | bytes 3145728 | tf_op jit(solution)/shard_map/project/pallas_call | solution.py:141
  7.6 1.5 %collective-permute-start.3 = (bf16[1024,256]{1,0:T(8,128)(2,1)}, bf16[1024,256]{1,0:T(8,128)(2,1)S(1)}, u32[]{:S(2)}, u32[]{:S(2)}) collective-permute-start(bf16[1024,256]{1,0:T(8,128)(2,1)} %refs_8_.1), channel_id=1, source_target_pairs={{32,0},{112,16},{64,32},{16,48},{96,64},{48,80},{0,96},{80,112},{3... | collective-permute-start | bytes 1572872 | tf_op jit(solution)/shard_map/ppermute | solution.py:399
  9.1 0.0 collective-permute-done.1.rest_1_
  9.1 3.7 %attend_0.1 = (f32[9,256,512]{2,1,0:T(8,128)S(1)}, f32[9,8,512]{2,1,0:T(8,128)S(1)}) custom-call(s32[8,128]{1,0:T(8,128)S(1)} %get-tuple-element.25.items, bf16[8,256,512]{2,1,0:T(8,128)(2,1)S(1)} %get-tuple-element.27.q_ref, bf16[1024,256]{1,0:T(8,128)(2,1)S(1)} %get-tuple-element.28.rest_0_, bf16[1024,256]{1,0:T(8,128)(2,1)S(1)} %collective-permute-done.1.rest_1_), custom_call_target="tpu_custom_call" | custom-call | flops 1000000000 | bytes 4194304 | tf_op jit(solution)/shard_map/attend_0/pallas_call | solution.py:281
  12.8 0.0 collective-permute-done.rest_0_.rest_2_
  12.8 0.2 collective-permute-start.4
  12.9 0.6 collective-permute-start.2
  13.5 4.6 %collective-permute-done.3.rest_1_.rest_3_ = bf16[1024,256]{1,0:T(8,128)(2,1)S(1)} collective-permute-done((bf16[1024,256]{1,0:T(8,128)(2,1)}, bf16[1024,256]{1,0:T(8,128)(2,1)S(1)}, u32[]{:S(2)}, u32[]{:S(2)}) %collective-permute-start.3) | collective-permute-done | bytes 524320 | tf_op jit(solution)/shard_map/ppermute | solution.py:399
  18.1 1.8 %collective-permute-start.6 = (bf16[1024,256]{1,0:T(8,128)(2,1)S(1)}, bf16[1024,256]{1,0:T(8,128)(2,1)S(1)}, u32[]{:S(2)}, u32[]{:S(2)}) collective-permute-start(bf16[1024,256]{1,0:T(8,128)(2,1)S(1)} %collective-permute-done.3.rest_1_.rest_3_), channel_id=1, source_target_pairs={{0,16},{16,0},{32,48},{48,32},{64,80},{80,64},{96,112},{112,96},{1... | collective-permute-start | bytes 1572872 | tf_op jit(solution)/shard_map/ppermute | solution.py:399
  19.9 0.0 collective-permute-done.4.rest_2_.rest_4_
  19.9 4.7 %attend_1.1 = (f32[9,256,512]{2,1,0:T(8,128)S(1)}, f32[9,8,512]{2,1,0:T(8,128)S(1)}) custom-call(s32[8,128]{1,0:T(8,128)S(1)} %get-tuple-element.25.items, bf16[8,256,512]{2,1,0:T(8,128)(2,1)S(1)} %get-tuple-element.27.q_ref, bf16[1024,256]{1,0:T(8,128)(2,1)S(1)} %collective-permute-done.rest_0_.rest_2_, ...), custom_call_target="tpu_custom_call", output_to_operand_aliasing={{0}: (5, {}), {1}: (6, {})} | custom-call | flops 1000000000 | bytes 4194304 | tf_op jit(solution)/shard_map/attend_1/pallas_call | solution.py:281
  24.6 0.0 collective-permute-done.2.rest_0_.rest_5_
  24.6 0.1 collective-permute-start.5
  24.7 0.0 collective-permute-done.6.rest_1_.rest_6_
  24.7 2.7 %attend_2.1 = (f32[9,256,512]{2,1,0:T(8,128)S(1)}, f32[9,8,512]{2,1,0:T(8,128)S(1)}) custom-call(s32[8,128]{1,0:T(8,128)S(1)} %get-tuple-element.25.items, bf16[8,256,512]{2,1,0:T(8,128)(2,1)S(1)} %get-tuple-element.27.q_ref, bf16[1024,256]{1,0:T(8,128)(2,1)S(1)} %collective-permute-done.2.rest_0_.rest_5_, ...), custom_call_target="tpu_custom_call", output_to_operand_aliasing={{0}: (4, {}), {1}: (5, {})} | custom-call | flops 1000000000 | bytes 4194304 | tf_op jit(solution)/shard_map/attend_2/pallas_call | solution.py:281
  27.5 0.0 collective-permute-done.5.rest_0_.rest_7_
  27.5 3.4 %attend_3.1 = (f32[9,256,512]{2,1,0:T(8,128)S(1)}, f32[9,8,512]{2,1,0:T(8,128)S(1)}, bf16[512,384]{1,0:T(8,128)(2,1)S(1)}) custom-call(s32[8,128]{1,0:T(8,128)S(1)} %get-tuple-element.25.items, bf16[8,256,512]{2,1,0:T(8,128)(2,1)S(1)} %get-tuple-element.27.q_ref, ...), custom_call_target="tpu_custom_call", output_to_operand_aliasing={{0}: (3, {}), {1}: (4, {})} | custom-call | flops 1000000000 | bytes 4194304 | tf_op jit(solution)/shard_map/attend_3/pallas_call | solution.py:281
  30.9 17.5 %all_to_all.10.got_ref = bf16[16,32,384]{2,1,0:T(8,128)(2,1)S(1)} all-to-all(bf16[16,32,384]{2,1,0:T(8,128)(2,1)S(1)} %bitcast.6), channel_id=1, replica_groups=mesh['query'=8,'space'=16] {'space'}, dimensions={0} | all-to-all | bytes 786432 | tf_op jit(solution)/shard_map/all_to_all | solution.py:420
  48.3 0.6 finish.1
  49.0 11.8 %all_to_all.11 = bf16[16,32,256]{2,1,0:T(8,128)(2,1)S(1)} all-to-all(bf16[16,32,256]{2,1,0:T(8,128)(2,1)S(1)} %finish.1), channel_id=1, replica_groups=mesh['query'=8,'space'=16] {'space'}, dimensions={0} | all-to-all | bytes 524288 | tf_op jit(solution)/shard_map/all_to_all | solution.py:422
  60.8 6.9 %logits.1 = (bf16[512,256]{1,0:T(8,128)(2,1)}, f32[512,8192]{1,0:T(8,128)}) custom-call(s32[2]{0:T(128)S(1)} %pad_add_fusion.place_ref, bf16[512,256]{1,0:T(8,128)(2,1)S(1)} %bitcast.7, bf16[256,256]{1,0:T(8,128)(2,1)S(1)} %get-tuple-element.47.wm, bf16[1024,256]{1,0:T(8,128)(2,1)S(1)} %get-tuple-element.28.rest_0_, ...), custom_call_target="tpu_custom_call" | custom-call | flops 2147483648 | bytes 20971520 | tf_op jit(solution)/shard_map/logits/pallas_call | solution.py:369
Async XLA Ops:
  0.6 8.5 %collective-permute-start.1 = (bf16[1024,256]{1,0:T(8,128)(2,1)}, bf16[1024,256]{1,0:T(8,128)(2,1)S(1)}, u32[]{:S(2)}, u32[]{:S(2)}) collective-permute-start(bf16[1024,256]{1,0:T(8,128)(2,1)} %refs_8_.1), channel_id=1, source_target_pairs={{0,16},{16,0},{32,48},{48,32},{64,80},{80,64},{96,112},{112,96},{1... | collective-permute-start | bytes 1572872 | tf_op jit(solution)/shard_map/ppermute | solution.py:399
  0.7 12.0 %collective-permute-start = (bf16[1024,256]{1,0:T(8,128)(2,1)}, bf16[1024,256]{1,0:T(8,128)(2,1)S(1)}, u32[]{:S(2)}, u32[]{:S(2)}) collective-permute-start(bf16[1024,256]{1,0:T(8,128)(2,1)} %refs_8_.1), channel_id=1, source_target_pairs={{0,32},{16,112},{32,64},{48,16},{64,96},{80,48},{96,0},{112,80},{1... | collective-permute-start | bytes 1572872 | tf_op jit(solution)/shard_map/ppermute | solution.py:399
  7.6 10.5 %collective-permute-start.3 = (bf16[1024,256]{1,0:T(8,128)(2,1)}, bf16[1024,256]{1,0:T(8,128)(2,1)S(1)}, u32[]{:S(2)}, u32[]{:S(2)}) collective-permute-start(bf16[1024,256]{1,0:T(8,128)(2,1)} %refs_8_.1), channel_id=1, source_target_pairs={{32,0},{112,16},{64,32},{16,48},{96,64},{48,80},{0,96},{80,112},{3... | collective-permute-start | bytes 1572872 | tf_op jit(solution)/shard_map/ppermute | solution.py:399
  12.8 7.2 %collective-permute-start.4 = (bf16[1024,256]{1,0:T(8,128)(2,1)S(1)}, bf16[1024,256]{1,0:T(8,128)(2,1)S(1)}, u32[]{:S(2)}, u32[]{:S(2)}) collective-permute-start(bf16[1024,256]{1,0:T(8,128)(2,1)S(1)} %collective-permute-done.rest_0_.rest_2_), channel_id=1, source_target_pairs={{0,16},{16,0},{32,48},{48,32},{64,80},{80,64},{96,112},{112,96},{1... | collective-permute-start | bytes 1572872 | tf_op jit(solution)/shard_map/ppermute | solution.py:399
  12.9 11.7 %collective-permute-start.2 = (bf16[1024,256]{1,0:T(8,128)(2,1)S(1)}, bf16[1024,256]{1,0:T(8,128)(2,1)S(1)}, u32[]{:S(2)}, u32[]{:S(2)}) collective-permute-start(bf16[1024,256]{1,0:T(8,128)(2,1)S(1)} %collective-permute-done.rest_0_.rest_2_), channel_id=1, source_target_pairs={{0,32},{16,112},{32,64},{48,16},{64,96},{80,48},{96,0},{112,80},{1... | collective-permute-start | bytes 1572872 | tf_op jit(solution)/shard_map/ppermute | solution.py:399
  18.1 6.6 %collective-permute-start.6 = (bf16[1024,256]{1,0:T(8,128)(2,1)S(1)}, bf16[1024,256]{1,0:T(8,128)(2,1)S(1)}, u32[]{:S(2)}, u32[]{:S(2)}) collective-permute-start(bf16[1024,256]{1,0:T(8,128)(2,1)S(1)} %collective-permute-done.3.rest_1_.rest_3_), channel_id=1, source_target_pairs={{0,16},{16,0},{32,48},{48,32},{64,80},{80,64},{96,112},{112,96},{1... | collective-permute-start | bytes 1572872 | tf_op jit(solution)/shard_map/ppermute | solution.py:399
  24.6 2.9 %collective-permute-start.5 = (bf16[1024,256]{1,0:T(8,128)(2,1)S(1)}, bf16[1024,256]{1,0:T(8,128)(2,1)S(1)}, u32[]{:S(2)}, u32[]{:S(2)}) collective-permute-start(bf16[1024,256]{1,0:T(8,128)(2,1)S(1)} %collective-permute-done.2.rest_0_.rest_5_), channel_id=1, source_target_pairs={{0,16},{16,0},{32,48},{48,32},{64,80},{80,64},{96,112},{112,96},{1... | collective-permute-start | bytes 1572872 | tf_op jit(solution)/shard_map/ppermute | solution.py:399
